TPU v7x, 256 devices: a whole 4x4x8 slice. The times are simulated.
256 devices in a mesh: tm: 128 (over z, x_lo, y, core), head: 2 (over x_hi).
Axes of the slice: x: 4 (x_hi: 2, x_lo: 2; x = x_hi * 2 + x_lo), y: 4, z: 8, core: 2. Of those that a mesh axis runs over, the one named last changes fastest.
Arguments:
- queries: bfloat16 [65536, 1024], P('tm', 'head'), may hold values from -16 to 16
- keys: bfloat16 [65536, 1024], P('tm', 'head'), may hold values from -16 to 16
- values: bfloat16 [65536, 1024], P('tm', 'head'), may hold values from -6 to 6
- grad_attn: bfloat16 [65536, 1024], P('tm', 'head'), may hold values from -128 to 128
- w_query: bfloat16 [1024, 1024], P(None, 'head'), may hold values from -0.1875 to 0.1875
- w_key: bfloat16 [1024, 1024], P(None, 'head'), may hold values from -0.1875 to 0.1875
- w_value: bfloat16 [1024, 1024], P(None, 'head'), may hold values from -0.1875 to 0.1875
Outputs:
- grad_frames: bfloat16 [65536, 1024], P(('tm', 'head'))
All inputs are finite; a program needn't handle non-finite values.
Results may differ from a plain program's by a relative error of at most 0.015.
Values may be sent and summed in bfloat16 or wider, within the bound.
No kernel may reach another device: no remote copies, remote signals or barrier semaphores. Data moves between devices by JAX's collectives and lax.ppermute only.
A program may use at most 128 MiB of HBM per device.

v0:
```python
import jax
import jax.numpy as jnp
from jax import lax
from jax.sharding import PartitionSpec as P

HEAD_DIM = 64


def from_partner(shard, axis, bit):
    return lax.ppermute(shard, axis, [(i, i ^ 1 << bit) for i in range(lax.axis_size(axis))])


def inner(former, latter):
    return lax.dot_general(
        former, latter, (((1,), (1,)), ((), ())), preferred_element_type=jnp.float32
    )


def outer_sum(former, latter):
    return lax.dot_general(
        former, latter, (((0,), (0,)), ((), ())), preferred_element_type=jnp.float32
    )


def head_cols(block, head_id):
    return lax.dynamic_slice_in_dim(block, head_id * HEAD_DIM, HEAD_DIM, 1)


def join_heads(stacked):
    return jnp.transpose(stacked, (1, 0, 2)).reshape(stacked.shape[1], -1)


def level_order(levels):
    return list(range(levels))


def upper_side(level):
    return jnp.bitwise_and(jnp.right_shift(lax.axis_index("tm"), level), 1) == 1


def place_pair(mine, arrived, level):
    return jnp.where(
        upper_side(level),
        jnp.concatenate([arrived, mine], axis=1),
        jnp.concatenate([mine, arrived], axis=1),
    )


def split_half(block, level):
    halfway = block.shape[1] // 2
    lower_part = block[:, :halfway]
    upper_part = block[:, halfway:]
    sending = jnp.where(upper_side(level), lower_part, upper_part)
    keeping = jnp.where(upper_side(level), upper_part, lower_part)
    return (sending, keeping)


def gather_groups(pieces, counts):
    pieces = list(pieces)
    for branch in range(len(pieces)):
        for level in level_order(counts[branch]):
            arrived = from_partner(pieces[branch], "tm", level)
            pieces[branch] = place_pair(pieces[branch], arrived, level)
    return pieces


def return_groups(pieces, counts):
    pieces = list(pieces)
    for branch in range(len(pieces)):
        for level in reversed(level_order(counts[branch])):
            outgoing, staying = split_half(pieces[branch], level)
            arrived = from_partner(outgoing.astype(jnp.bfloat16), "tm", level).astype(
                outgoing.dtype
            )
            pieces[branch] = staying + arrived
    return pieces


def branch_forward(query, key_block, value_block, score_scale):

    def per_head(head_id):
        scores = inner(head_cols(query, head_id), head_cols(key_block, head_id)) * score_scale
        highest = jnp.max(scores, axis=1)
        shifted = jnp.exp(scores - highest[:, None])
        totals = jnp.sum(shifted, axis=1)
        weighted = jnp.dot(
            shifted.astype(jnp.bfloat16),
            head_cols(value_block, head_id),
            preferred_element_type=jnp.float32,
        )
        return (highest, totals, weighted)

    return lax.map(per_head, jnp.arange(query.shape[1] // HEAD_DIM))


def branch_backward(query, key_block, value_block, grad_rows, lse_rows, delta_rows, score_scale):

    def per_head(head_id):
        query_head = head_cols(query, head_id)
        key_head = head_cols(key_block, head_id)
        value_head = head_cols(value_block, head_id)
        grad_head = head_cols(grad_rows, head_id)
        scores = inner(query_head, key_head) * score_scale
        probs = jnp.exp(scores - lse_rows[head_id][:, None])
        grad_value = outer_sum(probs.astype(jnp.bfloat16), grad_head)
        grad_prob = inner(grad_head, value_head)
        grad_score = (probs * (grad_prob - delta_rows[head_id][:, None])).astype(jnp.bfloat16)
        grad_query = jnp.dot(grad_score, key_head, preferred_element_type=jnp.float32) * score_scale
        grad_key = outer_sum(grad_score, query_head) * score_scale
        return (grad_query, grad_key, grad_value)

    grad_query, grad_key, grad_value = lax.map(per_head, jnp.arange(query.shape[1] // HEAD_DIM))
    return (join_heads(grad_query), jnp.stack([join_heads(grad_key), join_heads(grad_value)]))


def on_device(queries, keys, values, grad_attn, w_query, w_key, w_value):
    devices = lax.axis_size("tm")
    dilation_steps = [min(4, devices), min(16, devices), min(64, devices)]
    counts = [dilation.bit_length() - 1 for dilation in dilation_steps]
    score_scale = HEAD_DIM ** (-0.5)
    frames_here = queries.shape[0]
    heads_here = queries.shape[1] // HEAD_DIM
    pieces = [jnp.stack([keys[::dilation], values[::dilation]]) for dilation in dilation_steps]
    gathered = gather_groups(pieces, counts)
    highest, totals, weighted = branch_forward(queries, keys, values, score_scale)
    for branch, dilation in enumerate(dilation_steps):
        top_part, sum_part, acc_part = branch_forward(
            queries[::dilation], gathered[branch][0], gathered[branch][1], score_scale
        )
        old_top = highest[:, ::dilation]
        new_top = jnp.maximum(old_top, top_part)
        keep_old = jnp.exp(old_top - new_top)
        take_new = jnp.exp(top_part - new_top)
        totals = totals.at[:, ::dilation].set(
            totals[:, ::dilation] * keep_old + sum_part * take_new
        )
        weighted = weighted.at[:, ::dilation].set(
            weighted[:, ::dilation] * keep_old[:, :, None] + acc_part * take_new[:, :, None]
        )
        highest = highest.at[:, ::dilation].set(new_top)
    lse_all = highest + jnp.log(totals)
    attn = weighted / totals[:, :, None]
    grad_heads = jnp.transpose(
        grad_attn.reshape(frames_here, heads_here, HEAD_DIM), (1, 0, 2)
    ).astype(jnp.float32)
    delta = jnp.sum(attn * grad_heads, axis=2)
    grad_q, grad_kv = branch_backward(queries, keys, values, grad_attn, lse_all, delta, score_scale)
    partials = []
    for branch, dilation in enumerate(dilation_steps):
        part_q, part_kv = branch_backward(
            queries[::dilation],
            gathered[branch][0],
            gathered[branch][1],
            grad_attn[::dilation],
            lse_all[:, ::dilation],
            delta[:, ::dilation],
            score_scale,
        )
        grad_q = grad_q.at[::dilation].add(part_q)
        partials.append(part_kv)
    owned = return_groups(partials, counts)
    for branch, dilation in enumerate(dilation_steps):
        grad_kv = grad_kv.at[:, ::dilation].add(owned[branch])
    round_q = grad_q.astype(jnp.bfloat16)
    round_k = grad_kv[0].astype(jnp.bfloat16)
    round_v = grad_kv[1].astype(jnp.bfloat16)
    return lax.psum_scatter(
        (inner(round_q, w_query) + inner(round_k, w_key) + inner(round_v, w_value)).astype(
            jnp.bfloat16
        ),
        "head",
        scatter_dimension=0,
        tiled=True,
    )


def solution(mesh):
    return jax.shard_map(
        on_device,
        mesh=mesh,
        in_specs=(
            P("tm", "head"),
            P("tm", "head"),
            P("tm", "head"),
            P("tm", "head"),
            P(None, "head"),
            P(None, "head"),
            P(None, "head"),
        ),
        out_specs=P(("tm", "head"), None),
        check_vma=False,
    )
```

profile of v0, /device:TPU:1, one launch (start us, length us, event | category | flops | bytes accessed | tf_op | source)
XLA Modules:
  0.0 722.7 jit_solution(14020224491809714870)
XLA Ops:
  19.4 42.2 %while.112 = (s32[]{:T(128)}, f32[8,512]{1,0:T(8,128)S(1)}, f32[8,512]{1,0:T(8,128)}, f32[8,512,64]{1,2,0:T(8,128)S(1)}, s32[8]{0:T(128)S(1)}, /*index=5*/bf16[5...) while((s32[]{:T(128)}, f32[8,512]{1,0:T(8,128)S(1)}, ...), condition=%wide.region_3.4_spmd, body=%wide.region_0.3_spmd.sunk | while | flops 68680704 | bytes 3688123 | solution.py:93
  77.3 9.4 %slice.209 = f32[8,128,64]{1,2,0:T(8,128)} slice(f32[8,512,64]{1,2,0:T(8,128)S(1)} %get-tuple-element.425), slice={[0:8:1], [0:512:4], [0:64:1]} | slice | bytes 524288 | tf_op jit(solution)/shard_map/slice | solution.py:138
  115.3 36.5 %while.113 = (s32[]{:T(128)}, f32[8,128]{1,0:T(8,128)S(1)}, f32[8,128]{1,0:T(8,128)S(1)}, f32[8,128,64]{1,2,0:T(8,128)}, s32[8]{0:T(128)S(1)}, /*index=5*/bf16[1...) while((s32[]{:T(128)}, f32[8,128]{1,0:T(8,128)S(1)}, ...), condition=%wide.region_7.8_spmd, body=%wide.region_4.7_spmd.sunk | while | flops 17170180 | bytes 1119931 | solution.py:93
  165.5 8.8 %scatter_fusion.4 = f32[8,512,64]{2,0,1:T(8,128)S(1)} fusion(f32[8,512,64]{2,0,1:T(8,128)S(1)} %copy.145, s32[128]{0:T(128)} %multiply_bitcast_fusion.2, f32[128,8,64]{2,1,0:T(8,128)} %copy.146), kind=kCustom, calls=%fused_computation.6 | custom fusion | bytes 786944 | tf_op jit(solution)/shard_map/scatter | solution.py:137
  177.8 77.3 %while.114 = (s32[]{:T(128)}, f32[8,32]{1,0:T(8,128)}, f32[8,32]{1,0:T(8,128)}, f32[8,32,64]{2,0,1:T(8,128)}, s32[8]{0:T(128)}, /*index=5*/bf16[32,512]{1,0:T(8,...) while((s32[]{:T(128)}, f32[8,32]{1,0:T(8,128)}, ...), condition=%wide.region_12.13_spmd, body=%wide.region_9.12_spmd.sunk | while | flops 4292550 | bytes 494299 | solution.py:93
  270.2 43.3 %while.115 = (s32[]{:T(128)}, f32[8,8]{1,0:T(8,128)S(1)}, f32[8,8]{1,0:T(8,128)S(1)}, f32[8,8,64]{2,0,1:T(8,128)}, s32[8]{0:T(128)S(1)}, /*index=5*/bf16[8,512]{...) while((s32[]{:T(128)}, f32[8,8]{1,0:T(8,128)S(1)}, ...), condition=%wide.region_17.18_spmd, body=%wide.region_14.17_spmd.sunk | while | flops 1073142 | bytes 320959 | solution.py:93
  332.5 52.6 %while.119 = (s32[]{:T(128)}, f32[8,8,64]{2,1,0:T(8,128)}, f32[8,512,64]{1,2,0:T(8,128)S(1)}, f32[8,512,64]{1,2,0:T(8,128)}, s32[8]{0:T(128)S(1)}, /*index=5*/bf...) while((s32[]{:T(128)}, f32[8,8,64]{2,1,0:T(8,128)}, ...), condition=%wide.region_35.36_spmd, body=%wide.region_34.35_spmd.sunk | while | flops 2679305 | bytes 745861 | solution.py:112
  389.5 4.8 select_convert_fusion
  396.7 58.2 %while.118 = (s32[]{:T(128)}, f32[8,32,64]{2,1,0:T(8,128)}, f32[8,512,64]{1,2,0:T(8,128)}, f32[8,512,64]{1,2,0:T(8,128)}, s32[8]{0:T(128)S(1)}, /*index=5*/bf16[...) while((s32[]{:T(128)}, f32[8,32,64]{2,1,0:T(8,128)}, ...), condition=%wide.region_32.33_spmd, body=%wide.region_31.32_spmd.sunk | while | flops 10618889 | bytes 1004801 | solution.py:112
  454.8 3.7 copy.169
  460.5 4.9 select_convert_fusion.1
  468.9 52.0 %while.117 = (s32[]{:T(128)}, f32[8,128,64]{1,2,0:T(8,128)S(1)}, f32[8,512,64]{1,2,0:T(8,128)}, f32[8,512,64]{1,2,0:T(8,128)}, s32[8]{0:T(128)S(1)}, /*index=5*/...) while((s32[]{:T(128)}, f32[8,128,64]{1,2,0:T(8,128)S(1)}, ...), condition=%wide.region_29.30_spmd, body=%wide.region_28.29_spmd.sunk | while | flops 42377224 | bytes 2005253 | solution.py:112
  524.0 3.8 copy.168
  527.8 4.7 select_convert_fusion.2
  537.7 73.8 %while.116 = (s32[]{:T(128)}, f32[8,512,64]{1,2,0:T(8,128)}, f32[8,512,64]{1,2,0:T(8,128)}, f32[8,512,64]{1,2,0:T(8,128)}, s32[8]{0:T(128)S(1)}, /*index=5*/bf16...) while((s32[]{:T(128)}, f32[8,512,64]{1,2,0:T(8,128)}, ...), condition=%wide.region_27.28_spmd, body=%wide.region_26.27_spmd.sunk | while | flops 169410560 | bytes 6045441 | solution.py:112
  611.5 3.6 copy.165
  615.1 3.6 copy.166
  625.7 4.7 pad_maximum_fusion
  632.5 4.2 convert_add_fusion
  637.2 4.2 convert_add_fusion.1
  643.2 4.1 convert_add_fusion.2
  647.6 3.8 collective-permute-start.13
  656.4 10.8 %scatter_fusion.10 = f32[2,512,512]{2,0,1:T(2,128)S(1)} fusion(f32[2,512,512]{2,0,1:T(2,128)S(1)} %copy-done.4, s32[128]{0:T(128)S(1)} %copy-done.31, f32[128,2,512]{2,1,0:T(2,128)} %add_bitcast_fusion), kind=kCustom, calls=%fused_computation.12 | custom fusion | flops 131072 | bytes 1573376 | tf_op jit(solution)/shard_map/scatter-add | solution.py:163
  688.1 27.5 %reduce-scatter.2.cloned.1.call-done = bf16[256,1024]{1,0:T(8,128)(2,1)} async-done(((bf16[512,1024]{1,0:T(8,128)(2,1)}), bf16[256,1024]{1,0:T(8,128)(2,1)}) %reduce-scatter.2.cloned.1.call-update) | async-done | bytes 524304 | tf_op jit(solution)/shard_map/reduce_scatter | solution.py:167
  (722 shorter events, 503.4 us)
Async XLA Ops:
  6.5 709.1 %reduce-scatter.2.cloned.1.call-start = ((), (), s32[]{:S(2)}) async-start(), calls=%async_computation.1 | async-start | bytes 1572864 | tf_op jit(solution)/shard_map/reduce_scatter | solution.py:167
  10.7 61.5 %collective-permute-start = (bf16[2,128,512]{2,1,0:T(8,128)(2,1)S(1)}, bf16[2,128,512]{2,1,0:T(8,128)(2,1)}, u32[]{:S(2)}, u32[]{:S(2)}) collective-permute-start(bf16[2,128,512]{2,1,0:T(8,128)(2,1)S(1)} %pad_maximum_fusion.4), channel_id=1, source_target_pairs={{0,2},{2,0},{4,6},{6,4},{8,10},{10,8},{12,14},{14,12},{16,18},{18,... | collective-permute-start | bytes 786440 | tf_op jit(solution)/shard_map/ppermute | solution.py:10
  18.6 45.4 %collective-permute-start.2 = (bf16[2,32,512]{2,1,0:T(8,128)(2,1)S(1)}, bf16[2,32,512]{2,1,0:T(8,128)(2,1)S(1)}, u32[]{:S(2)}, u32[]{:S(2)}) collective-permute-start(bf16[2,32,512]{2,1,0:T(8,128)(2,1)S(1)} %pad_maximum_fusion.5), channel_id=1, source_target_pairs={{0,2},{2,0},{4,6},{6,4},{8,10},{10,8},{12,14},{14,12},{16,18},{18,... | collective-permute-start | bytes 196616 | tf_op jit(solution)/shard_map/ppermute | solution.py:10
  19.1 42.5 %collective-permute-start.7 = (bf16[2,16,512]{2,1,0:T(8,128)(2,1)S(1)}, bf16[2,16,512]{2,1,0:T(8,128)(2,1)S(1)}, u32[]{:S(2)}, u32[]{:S(2)}) collective-permute-start(bf16[2,16,512]{2,1,0:T(8,128)(2,1)S(1)} %maximum_select_fusion.11), channel_id=1, source_target_pairs={{0,4},{2,6},{4,0},{6,2},{8,12},{10,14},{12,8},{14,10},{16,20},{18,... | collective-permute-start | bytes 98312 | tf_op jit(solution)/shard_map/ppermute | solution.py:10
  61.7 5.4 collective-permute-start.8
  63.9 4.5 collective-permute-start.3
  68.0 6.2 collective-permute-start.9
  69.2 34.9 %collective-permute-start.4 = (bf16[2,128,512]{2,1,0:T(8,128)(2,1)}, bf16[2,128,512]{2,1,0:T(8,128)(2,1)}, u32[]{:S(2)}, u32[]{:S(2)}) collective-permute-start(bf16[2,128,512]{2,1,0:T(8,128)(2,1)} %maximum_select_fusion.6), channel_id=1, source_target_pairs={{0,8},{2,10},{4,12},{6,14},{8,0},{10,2},{12,4},{14,6},{16,24},{18,... | collective-permute-start | bytes 786440 | tf_op jit(solution)/shard_map/ppermute | solution.py:10
  74.2 37.5 %collective-permute-start.1 = (bf16[2,256,512]{2,1,0:T(8,128)(2,1)}, bf16[2,256,512]{2,1,0:T(8,128)(2,1)}, u32[]{:S(2)}, u32[]{:S(2)}) collective-permute-start(bf16[2,256,512]{2,1,0:T(8,128)(2,1)} %maximum_select_fusion.3), channel_id=1, source_target_pairs={{0,4},{2,6},{4,0},{6,2},{8,12},{10,14},{12,8},{14,10},{16,20},{18,... | collective-permute-start | bytes 1572872 | tf_op jit(solution)/shard_map/ppermute | solution.py:10
  75.0 31.6 %collective-permute-start.10 = (bf16[2,128,512]{2,1,0:T(8,128)(2,1)}, bf16[2,128,512]{2,1,0:T(8,128)(2,1)}, u32[]{:S(2)}, u32[]{:S(2)}) collective-permute-start(bf16[2,128,512]{2,1,0:T(8,128)(2,1)} %maximum_select_fusion.7), channel_id=1, source_target_pairs={{0,32},{2,34},{4,36},{6,38},{8,40},{10,42},{12,44},{14,46},{16,48}... | collective-permute-start | bytes 786440 | tf_op jit(solution)/shard_map/ppermute | solution.py:10
  106.2 68.2 %collective-permute-start.5 = (bf16[2,256,512]{2,1,0:T(8,128)(2,1)}, bf16[2,256,512]{2,1,0:T(8,128)(2,1)}, u32[]{:S(2)}, u32[]{:S(2)}) collective-permute-start(bf16[2,256,512]{2,1,0:T(8,128)(2,1)} %maximum_select_fusion.4), channel_id=1, source_target_pairs={{0,16},{2,18},{4,20},{6,22},{8,24},{10,26},{12,28},{14,30},{16,0},... | collective-permute-start | bytes 1572872 | tf_op jit(solution)/shard_map/ppermute | solution.py:10
  108.7 158.5 %collective-permute-start.11 = (bf16[2,256,512]{2,1,0:T(8,128)(2,1)}, bf16[2,256,512]{2,1,0:T(8,128)(2,1)}, u32[]{:S(2)}, u32[]{:S(2)}) collective-permute-start(bf16[2,256,512]{2,1,0:T(8,128)(2,1)} %maximum_select_fusion.5), channel_id=1, source_target_pairs={{0,64},{2,66},{4,68},{6,70},{8,72},{10,74},{12,76},{14,78},{16,80}... | collective-permute-start | bytes 1572872 | tf_op jit(solution)/shard_map/ppermute | solution.py:10
  394.3 238.2 %collective-permute-start.18 = (bf16[2,256,512]{2,0,1:T(2,128)(2,1)}, bf16[2,256,512]{2,0,1:T(2,128)(2,1)}, u32[]{:S(2)}, u32[]{:S(2)}) collective-permute-start(bf16[2,256,512]{2,0,1:T(2,128)(2,1)} %select_convert_fusion), channel_id=1, source_target_pairs={{0,64},{2,66},{4,68},{6,70},{8,72},{10,74},{12,76},{14,78},{16,80}... | collective-permute-start | bytes 1572872 | tf_op jit(solution)/shard_map/ppermute | solution.py:10
  465.4 171.8 %collective-permute-start.14 = (bf16[2,256,512]{2,0,1:T(2,128)(2,1)}, bf16[2,256,512]{2,0,1:T(2,128)(2,1)}, u32[]{:S(2)}, u32[]{:S(2)}) collective-permute-start(bf16[2,256,512]{2,0,1:T(2,128)(2,1)} %select_convert_fusion.1), channel_id=1, source_target_pairs={{0,16},{2,18},{4,20},{6,22},{8,24},{10,26},{12,28},{14,30},{16,0},... | collective-permute-start | bytes 1572872 | tf_op jit(solution)/shard_map/ppermute | solution.py:10
  532.5 110.7 %collective-permute-start.12 = (bf16[2,256,512]{2,0,1:T(2,128)(2,1)}, bf16[2,256,512]{2,0,1:T(2,128)(2,1)}, u32[]{:S(2)}, u32[]{:S(2)}) collective-permute-start(bf16[2,256,512]{2,0,1:T(2,128)(2,1)} %select_convert_fusion.2), channel_id=1, source_target_pairs={{0,4},{2,6},{4,0},{6,2},{8,12},{10,14},{12,8},{14,10},{16,20},{18,... | collective-permute-start | bytes 1572872 | tf_op jit(solution)/shard_map/ppermute | solution.py:10
  637.0 14.4 %collective-permute-start.19 = (bf16[2,128,512]{2,0,1:T(2,128)(2,1)S(1)}, bf16[2,128,512]{2,0,1:T(2,128)(2,1)S(1)}, u32[]{:S(2)}, u32[]{:S(2)}) collective-permute-start(bf16[2,128,512]{2,0,1:T(2,128)(2,1)S(1)} %select_convert_fusion.3), channel_id=1, source_target_pairs={{0,32},{2,34},{4,36},{6,38},{8,40},{10,42},{12,44},{14,46},{16,48}... | collective-permute-start | bytes 786440 | tf_op jit(solution)/shard_map/ppermute | solution.py:10
  641.6 11.9 %collective-permute-start.15 = (bf16[2,128,512]{2,0,1:T(2,128)(2,1)S(1)}, bf16[2,128,512]{2,0,1:T(2,128)(2,1)S(1)}, u32[]{:S(2)}, u32[]{:S(2)}) collective-permute-start(bf16[2,128,512]{2,0,1:T(2,128)(2,1)S(1)} %select_convert_fusion.4), channel_id=1, source_target_pairs={{0,8},{2,10},{4,12},{6,14},{8,0},{10,2},{12,4},{14,6},{16,24},{18,... | collective-permute-start | bytes 786440 | tf_op jit(solution)/shard_map/ppermute | solution.py:10
  647.6 7.7 %collective-permute-start.13 = (bf16[2,128,512]{2,0,1:T(2,128)(2,1)S(1)}, bf16[2,128,512]{2,0,1:T(2,128)(2,1)S(1)}, u32[]{:S(2)}, u32[]{:S(2)}) collective-permute-start(bf16[2,128,512]{2,0,1:T(2,128)(2,1)S(1)} %select_convert_fusion.5), channel_id=1, source_target_pairs={{0,2},{2,0},{4,6},{6,4},{8,10},{10,8},{12,14},{14,12},{16,18},{18,... | collective-permute-start | bytes 786440 | tf_op jit(solution)/shard_map/ppermute | solution.py:10
  652.7 14.5 %collective-permute-start.20 = (bf16[2,64,512]{2,0,1:T(2,128)(2,1)}, bf16[2,64,512]{2,0,1:T(2,128)(2,1)S(1)}, u32[]{:S(2)}, u32[]{:S(2)}) collective-permute-start(bf16[2,64,512]{2,0,1:T(2,128)(2,1)} %select_convert_fusion.6), channel_id=1, source_target_pairs={{0,16},{2,18},{4,20},{6,22},{8,24},{10,26},{12,28},{14,30},{16,0},... | collective-permute-start | bytes 393224 | tf_op jit(solution)/shard_map/ppermute | solution.py:10
  654.0 16.1 %collective-permute-start.16 = (bf16[2,64,512]{2,0,1:T(2,128)(2,1)S(1)}, bf16[2,64,512]{2,0,1:T(2,128)(2,1)S(1)}, u32[]{:S(2)}, u32[]{:S(2)}) collective-permute-start(bf16[2,64,512]{2,0,1:T(2,128)(2,1)S(1)} %select_convert_fusion.7), channel_id=1, source_target_pairs={{0,4},{2,6},{4,0},{6,2},{8,12},{10,14},{12,8},{14,10},{16,20},{18,... | collective-permute-start | bytes 393224 | tf_op jit(solution)/shard_map/ppermute | solution.py:10
  668.5 4.7 collective-permute-start.21
  673.3 3.1 collective-permute-start.22
  674.0 5.4 collective-permute-start.17
  676.5 4.9 collective-permute-start.23
  (44 other events, 857.5 us)
Sparse Core Ops, SparseCore 0:
  688.2 27.3 reduce-scatter.1
where the time goes:
time: 737 us; the launch traced here: 723 us
  local copies, waits for them, and re-layouts  227 us (31%)
  matrix products  221 us (30%)
  other arithmetic  98.1 us (13%)
  loops' own time  98.1 us (13%)
  starting transfers between devices  32.3 us (4%)
  waiting for transfers between devices  32 us (4%)
  between operations  14.4 us (2%)
    dot_general x99, matrix products, inner(): lax.dot_general(former, latter, (((1,), (1,)), ((), ())), preferred_eleme...  92.7 us
    another operation x4, loops' own time, branch_backward(): lax.map(per_head, jnp.arange(query.shape[1] // HEAD_DIM))  77.6 us
    dot_general x64, matrix products, outer_sum(): lax.dot_general(former, latter, (((0,), (0,)), ((), ())), preferred_eleme...  62.5 us
    dynamic_update_slice x80, local copies, waits for them, and re-layouts, branch_forward(): return lax.map(per_head, jnp.arange(query.shape[1] // HEAD_DIM))  56.7 us
    dynamic_slice x64, local copies, waits for them, and re-layouts, branch_forward(): return lax.map(per_head, jnp.arange(query.shape[1] // HEAD_DIM))  43.5 us
    dot_general x32, matrix products, per_head(): jnp.dot(shifted.astype(jnp.bfloat16), head_cols(value_block, head_id), pr...  42.4 us
    ppermute x24, starting transfers between devices, from_partner(): lax.ppermute(shard, axis, [(i, i ^ 1 << bit) for i in range(lax.axis_size...  32.3 us
    reduce_scatter x1, waiting for transfers between devices, on_device(): lax.psum_scatter((inner(round_q, w_query) + inner(round_k, w_key) + inner...  27.5 us
  transfers between devices with their start and end apart: 25, of which 4 were waited for; matrix products, arithmetic and copies ran while one was open for 59% of the time, Pallas kernels for 0%

commit v1 on v0

v1 whole, which is shorter than its diff:
```python
import functools

import jax
import jax.numpy as jnp
import numpy as np
from jax import lax
from jax.experimental import pallas as pl
from jax.experimental.pallas import tpu as pltpu
from jax.sharding import PartitionSpec as P

BF16 = jnp.bfloat16
F32 = jnp.float32
ROWS = 512
DIL = 128
REST = ROWS - DIL
LANES = 128
HEADS = 8
STAT_ROWS = 16
VMEM = 48 * 1024 * 1024
LOW = -1e30


def frame_order():
    r = np.arange(DIL)
    dil = np.concatenate([r[r % 16 == 0], r[(r % 4 == 0) & (r % 16 != 0)], r[r % 4 != 0]])
    f = np.arange(ROWS)
    return dil, np.concatenate([dil * 4, f[f % 4 != 0]])


def one_hot(index, width):
    out = np.zeros((len(index), width), np.float32)
    out[np.arange(len(index)), index] = 1
    return out


def dot_tt(a, b):
    return lax.dot_general(a, b, (((1,), (1,)), ((), ())), preferred_element_type=F32)


def dot(a, b):
    return jnp.dot(a, b, preferred_element_type=F32)


def half_mask(side):
    lane = lax.broadcasted_iota(jnp.int32, (1, LANES), 1)
    return jnp.where((lane >= 64) == (side == 1), 1.0, 0.0)


def choose(first, second):
    lane = lax.broadcasted_iota(jnp.int32, first.shape, 1)
    return jnp.where(lane < 64, first, second)


def stats(scores, grad_prob):
    top = jnp.max(scores, axis=0, keepdims=True)
    e = jnp.exp(scores - top)
    total = jnp.sum(e, axis=0, keepdims=True)
    delta = jnp.sum(e * grad_prob, axis=0, keepdims=True) / total
    return e, total, top + jnp.log(total), delta


def thirds(x):
    a = x.astype(BF16).astype(F32)
    b = (x - a).astype(BF16).astype(F32)
    return [a, b, x - a - b]


def pack_kernel(perm_ref, q_ref, k_ref, v_ref, g_ref, qo, ko, vo, go, x_ref):
    block = jnp.concatenate([q_ref[...] * BF16(0.125), k_ref[...], v_ref[...], g_ref[...]], axis=1)
    block = dot(perm_ref[...], block).astype(BF16)
    q, k, v, g = (block[:, i * LANES : (i + 1) * LANES] for i in range(4))
    qo[...] = q
    ko[...] = k
    vo[...] = v
    go[...] = g
    for h in range(2):
        mask = half_mask(h).astype(BF16)
        scores = dot_tt(k * mask, q[:DIL])
        grad_prob = dot_tt(v * mask, g[:DIL])
        _, _, lse, delta = stats(scores, grad_prob)
        rows = jnp.concatenate(thirds(lse) + thirds(delta) + [jnp.zeros((STAT_ROWS - 6, LANES), F32)], axis=0)
        cols = slice(h * 64, h * 64 + 64)
        x_ref[h, :DIL, :] = jnp.concatenate([k[:DIL, cols], v[:DIL, cols], q[:DIL, cols], g[:DIL, cols]], axis=1)
        x_ref[h, DIL:, :] = jnp.concatenate([rows, jnp.zeros_like(rows)], axis=1).astype(BF16)


def local_kernel(q_ref, k_ref, v_ref, g_ref, dq_ref, dk_ref, dv_ref):
    q, g = q_ref[DIL:, :], g_ref[DIL:, :]
    k, v = k_ref[...], v_ref[...]
    dq, dk, dv = None, [], []
    for h in range(2):
        mask = half_mask(h).astype(BF16)
        km = k * mask
        scores = dot_tt(km, q)
        grad_prob = dot_tt(v * mask, g)
        e, total, _, delta = stats(scores, grad_prob)
        p = e * (1.0 / total)
        ds = (p * (grad_prob - delta)).astype(BF16)
        dv.append(dot(p.astype(BF16), g))
        dk.append(dot(ds, q))
        part = dot((km * BF16(0.125)).T, ds)
        dq = part if dq is None else dq + part
    dk_ref[...] = choose(*dk)
    dv_ref[...] = choose(*dv)
    dq_ref[...] = dq.T.astype(BF16)


def head_kernel(x_ref, p16_ref, c64_ref, own_ref, dq_ref, part16_ref, part64_ref, stat_ref):
    first = half_mask(0).astype(BF16)
    second = half_mask(1).astype(BF16)

    def products(kv, qg):
        return dot_tt(kv * first, qg), dot_tt(kv * second, qg)

    def grads(kv, qg, scores, grad_prob, lse, delta):
        p = jnp.exp(scores - lse)
        ds = (p * (grad_prob - delta)).astype(BF16)
        dkv = choose(dot(ds, qg), dot(p.astype(BF16), qg))
        dq = dot((kv * (first * BF16(0.125))).T, ds).T
        return dkv, dq

    def spread(row, width, fill):
        lines = []
        for s in range(HEADS):
            piece = row[:, s * width : (s + 1) * width]
            if width < DIL:
                piece = jnp.concatenate([piece, jnp.full((1, DIL - width), fill, F32)], axis=1)
            lines.append(piece)
        return jnp.concatenate(lines, axis=0)

    def collect(table, width):
        return jnp.concatenate([table[s : s + 1, :width] for s in range(HEADS)], axis=1)

    segments = []
    for s in range(2):
        block = x_ref[4 * s : 4 * s + 4, :DIL, :].reshape(4 * DIL, 2 * LANES)
        segments.append((block[:, :LANES], block[:, LANES:]))
    block16 = x_ref[:, :32, :].reshape(256, 2 * LANES)
    kv16 = jnp.concatenate([block16[:, :LANES], p16_ref[...]], axis=0)
    qg16 = block16[:, LANES:]
    qg64 = x_ref[:, :16, LANES:].astype(F32)[:, :8, :].reshape(64, LANES).astype(BF16)
    kv64 = c64_ref[...].reshape(512, LANES)

    lse1, delta1 = [], []
    for s in range(HEADS):
        rows = x_ref[s, DIL:, :LANES].astype(F32)
        lse1.append(rows[0:1] + rows[1:2] + rows[2:3])
        delta1.append(rows[3:4] + rows[4:5] + rows[5:6])
    lses = [jnp.concatenate(lse1, axis=0)]
    deltas = [jnp.concatenate(delta1, axis=0)]

    made = [products(kv, qg) for kv, qg in segments]
    got = [stats(*pair) for pair in made]
    lses.append(spread(jnp.concatenate([got[0][2], got[1][2]], axis=1), DIL, LOW))
    deltas.append(spread(jnp.concatenate([got[0][3], got[1][3]], axis=1), DIL, 0.0))
    made16 = products(kv16, qg16)
    got = stats(*made16)
    lses.append(spread(got[2], 32, LOW))
    deltas.append(spread(got[3], 32, 0.0))
    made64 = products(kv64, qg64)
    got = stats(*made64)
    lses.append(spread(got[2], 8, LOW))
    deltas.append(spread(got[3], 8, 0.0))

    top = functools.reduce(jnp.maximum, lses)
    parts = [jnp.exp(x - top) for x in lses]
    total = sum(parts)
    lse = top + jnp.log(total)
    delta = sum(w * d for w, d in zip(parts, deltas)) / total
    stat_ref[0] = lse
    stat_ref[1] = delta

    for s in range(2):
        row = [jnp.concatenate([t[4 * s + i : 4 * s + i + 1] for i in range(4)], axis=1) for t in (lse, delta)]
        dkv, dq = grads(*segments[s], *made[s], *row)
        own_ref[4 * s : 4 * s + 4] = dkv.reshape(4, DIL, LANES)
        dq_ref[4 * s : 4 * s + 4] = dq.reshape(4, DIL, LANES)
    dkv, dq = grads(kv16, qg16, *made16, collect(lse, 32), collect(delta, 32))
    own_ref[:, :32, :] = own_ref[:, :32, :] + dkv[:256].reshape(HEADS, 32, LANES)
    part16_ref[...] = dkv[256:].astype(BF16)
    dq_ref[:, :32, :] = dq_ref[:, :32, :] + dq.reshape(HEADS, 32, LANES)
    dkv, dq = grads(kv64, qg64, *made64, collect(lse, 8), collect(delta, 8))
    part64_ref[...] = dkv.reshape(HEADS, 64, LANES).astype(BF16)
    dq_ref[:, :8, :] = dq_ref[:, :8, :] + dq.reshape(HEADS, 8, LANES)


def gather_kernel(own_ref, dq_ref, got16_ref, got64_ref, out_ref):
    got16 = got16_ref[...].astype(F32).reshape(HEADS, 32, LANES)
    got64 = got64_ref[...].astype(F32)
    got64 = sum(got64[i] for i in range(HEADS)).reshape(HEADS, 8, LANES)
    first = got16[:, :8] + got64
    dkv = own_ref[...]
    dkv = jnp.concatenate([dkv[:, :8] + first, dkv[:, 8:32] + got16[:, 8:], dkv[:, 32:]], axis=1)
    out_ref[:, :DIL, :] = dkv.astype(BF16)
    for s in range(HEADS):
        dq = dq_ref[s]
        out_ref[s, DIL:, :] = jnp.concatenate([dq[:64, :64], dq[64:, :64]], axis=1).astype(BF16)


def rest_kernel(
    place_ref, q_ref, k_ref, v_ref, g_ref, dq1_ref, dk1_ref, dv1_ref, st_ref, wq_ref, wk_ref, wv_ref,
    dil_ref, keep_ref, send_ref, dq_s, dk_s, dv_s, out_s,
):
    slab = pl.program_id(0)
    line = place_ref[0]
    head = place_ref[1]
    q, g = q_ref[:DIL, :], g_ref[:DIL, :]
    k, v = k_ref[...], v_ref[...]
    dq, dk, dv = None, [], []
    for h in range(2):
        mask = half_mask(h).astype(BF16)
        km = k * mask
        scores = dot_tt(km, q)
        grad_prob = dot_tt(v * mask, g)
        at = jnp.bitwise_xor(2 * slab + h, line)
        lse = st_ref[at, 0, pl.ds(line, 1), :]
        delta = st_ref[at, 1, pl.ds(line, 1), :]
        p = jnp.exp(scores - lse)
        ds = (p * (grad_prob - delta)).astype(BF16)
        dv.append(dot(p.astype(BF16), g))
        dk.append(dot(ds, q))
        part = dot((km * BF16(0.125)).T, ds)
        dq = part if dq is None else dq + part
    dk = choose(*dk) + dk1_ref[...]
    dv = choose(*dv) + dv1_ref[...]
    dil_ref[0] = dq.T
    dil_ref[1] = dk[:DIL]
    dil_ref[2] = dv[:DIL]
    for s in range(4):

        @pl.when(slab == s)
        def _():
            cols = slice(s * LANES, (s + 1) * LANES)
            dq_s[:, cols] = dq1_ref[...]
            dk_s[:, cols] = dk[DIL:].astype(BF16)
            dv_s[:, cols] = dv[DIL:].astype(BF16)

    @pl.when(slab == 3)
    def _():
        out_s[...] = dot_tt(dq_s[...], wq_ref[...]) + dot_tt(dk_s[...], wk_ref[...]) + dot_tt(dv_s[...], wv_ref[...])
        half = REST // 2
        keep_ref[...] = out_s[pl.ds(pl.multiple_of(head * half, half), half), :]
        send_ref[...] = out_s[pl.ds(pl.multiple_of((1 - head) * half, half), half), :].astype(BF16)


def dil_kernel(place_ref, perm_ref, got_ref, dil_ref, wq_ref, wk_ref, wv_ref, keep_ref, send_ref, out_s):
    head = place_ref[1]

    def both(pieces):
        return jnp.concatenate(pieces, axis=1)

    dk = both([got_ref[h, :DIL, :64].astype(F32) for h in range(HEADS)])
    dv = both([got_ref[h, :DIL, 64:].astype(F32) for h in range(HEADS)])
    dq = jnp.concatenate(
        [both([got_ref[h, DIL:, s * 64 : s * 64 + 64].astype(F32) for h in range(HEADS)]) for s in range(2)], axis=0
    )
    perm = perm_ref[...]
    out = None
    for grad, i, w_ref in ((dq, 0, wq_ref), (dk, 1, wk_ref), (dv, 2, wv_ref)):
        rows = dot(perm, (grad + dil_ref[i]).astype(BF16)).astype(BF16)
        part = dot_tt(rows, w_ref[...])
        out = part if out is None else out + part
    out_s[...] = out
    half = DIL // 2
    keep_ref[...] = out_s[pl.ds(pl.multiple_of(head * half, half), half), :]
    send_ref[...] = out_s[pl.ds(pl.multiple_of((1 - head) * half, half), half), :].astype(BF16)


def last_kernel(perm_ref, keep_d, got_d, keep_r, got_r, out_ref):
    rows = jnp.concatenate(
        [keep_d[...] + got_d[...].astype(F32), keep_r[...] + got_r[...].astype(F32)], axis=0
    ).astype(BF16)
    out_ref[...] = dot(perm_ref[...], rows).astype(BF16)


def params():
    return pltpu.CompilerParams(vmem_limit_bytes=VMEM)


def cost(flops, bytes_accessed, exps):
    return pl.CostEstimate(flops=flops, bytes_accessed=bytes_accessed, transcendentals=exps)


def shape(dims, dtype):
    return jax.ShapeDtypeStruct(dims, dtype)


def slab_spec(rows):
    return pl.BlockSpec((rows, LANES), lambda s: (0, s))


def whole(dims):
    return pl.BlockSpec(dims, lambda s: (0,) * len(dims))


def swap(x, axis, bits):
    return lax.ppermute(x, axis, [(i, i ^ bits) for i in range(lax.axis_size(axis))])


def on_device(queries, keys, values, grad_attn, w_query, w_key, w_value):
    size = lax.axis_size("tm")
    lines = [[a * 8 + j for j in range(8)] for a in range(size // 8)]
    across = [[b * 64 + a * 8 + j for a in range(8)] for b in range(size // 64) for j in range(8)]
    smem = pl.BlockSpec(memory_space=pltpu.SMEM)
    place = jnp.stack([lax.rem(lax.axis_index("tm"), 8), lax.axis_index("head")]).astype(jnp.int32)
    dil, order = frame_order()
    perm = jnp.asarray(one_hot(order, ROWS), BF16)
    perm_dil = jnp.asarray(one_hot(np.argsort(dil), DIL), BF16)
    f = np.arange(256)
    seat = np.where(f % 4 == 0, f // 4, 64 + f - f // 4 - 1)
    perm_last = jnp.asarray(one_hot(seat, 256), BF16)

    block = shape((ROWS, 512), BF16)
    qp, kp, vp, gp, sent = pl.pallas_call(
        pack_kernel,
        grid=(4,),
        in_specs=[whole((ROWS, ROWS))] + [slab_spec(ROWS)] * 4,
        out_specs=[slab_spec(ROWS)] * 4 + [pl.BlockSpec((2, DIL + STAT_ROWS, 256), lambda s: (s, 0, 0))],
        out_shape=[block] * 4 + [shape((HEADS, DIL + STAT_ROWS, 256), BF16)],
        compiler_params=params(),
        name="pack",
    )(perm, queries, keys, values, grad_attn)

    x = lax.all_to_all(sent, "tm", 0, 0, axis_index_groups=lines, tiled=True)
    dq1, dk1, dv1 = pl.pallas_call(
        local_kernel,
        grid=(4,),
        in_specs=[slab_spec(ROWS)] * 4,
        out_specs=[slab_spec(REST), slab_spec(ROWS), slab_spec(ROWS)],
        out_shape=[shape((REST, 512), BF16), shape((ROWS, 512), F32), shape((ROWS, 512), F32)],
        compiler_params=params(),
        cost_estimate=cost(12_000_000_000, 5_000_000, 1_600_000),
        name="local",
    )(qp, kp, vp, gp)

    p16 = swap(x[:, :32, :LANES].reshape(256, LANES), "tm", 8)
    mine64 = x[:, :8, :LANES].reshape(64, LANES)
    c64 = lax.all_to_all(jnp.broadcast_to(mine64, (8, 64, LANES)), "tm", 0, 0, axis_index_groups=across, tiled=True)
    own, dq_own, part16, part64, stat = pl.pallas_call(
        head_kernel,
        out_shape=[
            shape((HEADS, DIL, LANES), F32),
            shape((HEADS, DIL, LANES), F32),
            shape((256, LANES), BF16),
            shape((8, 64, LANES), BF16),
            shape((2, HEADS, DIL), F32),
        ],
        compiler_params=params(),
        name="heads",
    )(x, p16, c64)

    st = stat[None]
    for bit in (1, 2, 4):
        st = jnp.concatenate([st, swap(st, "tm", bit)], axis=0)
    got16 = swap(part16, "tm", 8)
    got64 = lax.all_to_all(part64, "tm", 0, 0, axis_index_groups=across, tiled=True)
    back = pl.pallas_call(
        gather_kernel,
        out_shape=shape((HEADS, DIL + 64, LANES), BF16),
        compiler_params=params(),
        name="gather",
    )(own, dq_own, got16, got64)
    got = lax.all_to_all(back, "tm", 0, 0, axis_index_groups=lines, tiled=True)

    half = REST // 2
    dil_own, keep_r, send_r = pl.pallas_call(
        rest_kernel,
        grid=(4,),
        in_specs=[smem]
        + [slab_spec(ROWS)] * 4
        + [slab_spec(REST), slab_spec(ROWS), slab_spec(ROWS), whole((8, 2, HEADS, DIL))]
        + [whole((1024, 512))] * 3,
        out_specs=[pl.BlockSpec((3, DIL, LANES), lambda s: (0, 0, s)), whole((half, 1024)), whole((half, 1024))],
        out_shape=[shape((3, DIL, 512), F32), shape((half, 1024), F32), shape((half, 1024), BF16)],
        scratch_shapes=[pltpu.VMEM((REST, 512), BF16)] * 3 + [pltpu.VMEM((REST, 1024), F32)],
        compiler_params=params(),
        cost_estimate=cost(5_000_000_000, 9_000_000, 600_000),
        name="rest",
    )(place, qp, kp, vp, gp, dq1, dk1, dv1, st, w_query, w_key, w_value)
    got_r = swap(send_r, "head", 1)

    vmem = pl.BlockSpec(memory_space=pltpu.VMEM)
    keep_d, send_d = pl.pallas_call(
        dil_kernel,
        in_specs=[smem] + [vmem] * 6,
        out_shape=[shape((DIL // 2, 1024), F32), shape((DIL // 2, 1024), BF16)],
        scratch_shapes=[pltpu.VMEM((DIL, 1024), F32)],
        compiler_params=params(),
        name="dil",
    )(place, perm_dil, got, dil_own, w_query, w_key, w_value)
    got_d = swap(send_d, "head", 1)
    return pl.pallas_call(
        last_kernel,
        out_shape=shape((256, 1024), BF16),
        compiler_params=params(),
        name="last",
    )(perm_last, keep_d, got_d, keep_r, got_r)


def solution(mesh):
    return jax.shard_map(
        on_device,
        mesh=mesh,
        in_specs=(
            P("tm", "head"),
            P("tm", "head"),
            P("tm", "head"),
            P("tm", "head"),
            P(None, "head"),
            P(None, "head"),
            P(None, "head"),
        ),
        out_specs=P(("tm", "head"), None),
        check_vma=False,
    )
```

time: 737 us -> 110 us (0.15); the launches traced: 723 us -> 108 us
  matrix products: 221 us -> 0 us
  local copies, waits for them, and re-layouts: 227 us -> 21.4 us
  loops' own time: 98.1 us -> 0 us
  other arithmetic: 98.1 us -> 0.71 us
  Pallas kernels: 0 us -> 28.8 us
  blocking collectives: 0 us -> 16.1 us
  waiting for transfers between devices: 32 us -> 16.1 us
  between operations: 14.4 us -> 0.13 us
    dot_general x227 -> x0, matrix products: 221 us -> none  [the longest x99 92.7 us: inner(): lax.dot_general(former, latter, (((1,), (1,)), ((), ())), preferred_eleme...]
    another operation x8 -> x0, loops' own time: 98.1 us -> none  [the longest x4 77.6 us: branch_backward(): lax.map(per_head, jnp.arange(query.shape[1] // HEAD_DIM))]
    dynamic_update_slice x80 -> x0, local copies, waits for them, and re-layouts: 56.7 us -> none  [branch_forward(): return lax.map(per_head, jnp.arange(query.shape[1] // HEAD_DIM))]
    dynamic_slice x72 -> x0, local copies, waits for them, and re-layouts: 49.4 us -> none  [the longest x64 43.5 us: branch_forward(): return lax.map(per_head, jnp.arange(query.shape[1] // HEAD_DIM))]
    slice x26 -> x1, local copies, waits for them, and re-layouts: 36 us -> 0.01 us  [on_device(): p16 = swap(x[:, :32, :LANES].reshape(256, LANES), 'tm', 8)]
    another operation x20 -> x0, local copies, waits for them, and re-layouts: 33.5 us -> none  [the longest x8 23.5 us: branch_backward(): jnp.stack([join_heads(grad_key), join_heads(grad_value)])]
    pallas_call x0 -> x7, Pallas kernels: none -> 28.8 us  [the longest x1 8.18 us: on_device(): pl.pallas_call(rest_kernel, grid=(4,), in_specs=[smem] + [slab_spec(ROWS)...]
    reduce_scatter x1 -> x0, waiting for transfers between devices: 27.5 us -> none  [on_device(): lax.psum_scatter((inner(round_q, w_query) + inner(round_k, w_key) + inner...]
  transfers between devices with their start and end apart: 25 -> 10, of which waited for: 4 -> 8; matrix products, arithmetic and copies ran while one was open for 59% -> 1% of each run, Pallas kernels for 0% -> 17%
where the time goes in v1:
time: 110 us; the launch traced here: 108 us
  Pallas kernels  28.8 us (26%)
  starting transfers between devices  25.1 us (23%)
  local copies, waits for them, and re-layouts  21.4 us (19%)
  blocking collectives  16.1 us (15%)
  waiting for transfers between devices  16.1 us (15%)
    unnamed x58, local copies, waits for them, and re-layouts  20.7 us
    all_to_all x1, blocking collectives, on_device(): x = lax.all_to_all(sent, 'tm', 0, 0, axis_index_groups=lines, tiled=True)  16.1 us
    ppermute x7, waiting for transfers between devices, swap(): lax.ppermute(x, axis, [(i, i ^ bits) for i in range(lax.axis_size(axis))])  12.7 us
    ppermute x7, starting transfers between devices, swap(): lax.ppermute(x, axis, [(i, i ^ bits) for i in range(lax.axis_size(axis))])  10.2 us
    pallas_call x1, Pallas kernels, on_device(): pl.pallas_call(rest_kernel, grid=(4,), in_specs=[smem] + [slab_spec(ROWS)...  8.18 us
    pallas_call x1, Pallas kernels, on_device(): pl.pallas_call(local_kernel, grid=(4,), in_specs=[slab_spec(ROWS)] * 4, o...  7.83 us
    all_to_all x1, starting transfers between devices, on_device(): lax.all_to_all(jnp.broadcast_to(mine64, (8, 64, LANES)), 'tm', 0, 0, axis...  6.55 us
    all_to_all x1, starting transfers between devices, on_device(): got = lax.all_to_all(back, 'tm', 0, 0, axis_index_groups=lines, tiled=True)  5.02 us
  transfers between devices with their start and end apart: 10, of which 8 were waited for; matrix products, arithmetic and copies ran while one was open for 1% of the time, Pallas kernels for 17%

profile of v1, /device:TPU:1, one launch (start us, length us, event | category | flops | bytes accessed | tf_op | source)
XLA Modules:
  0.0 108.3 jit_solution(16883397203252661812)
XLA Ops:
  1.0 1.0 copy-done.8
  2.1 1.0 copy-done.9
  5.2 3.9 %pack.1 = (bf16[512,512]{1,0:T(8,128)(2,1)S(1)}, bf16[512,512]{1,0:T(8,128)(2,1)S(1)}, bf16[512,512]{1,0:T(8,128)(2,1)S(1)}, bf16[512,512]{1,0:T(8,128)(2,1)S(1)}, bf16[8,144,256]{2,1,0:T(8,128)(2,1)S(1)}) custom-call(bf16[512,512]{1,0:T(8,128)(2,1)S(1)} %copy-done.11, bf16[512,512]{1,0:T(8,128)(2,1)S(1)} %copy-done.7, bf16[512,512]{1,0:T(8,128)(2,1)S(1)} %copy-done.8, ...), custom_call_target="tpu_custom_call" | custom-call | tf_op jit(solution)/shard_map/pack/pallas_call | solution.py:314
  9.9 16.1 %all_to_all.20.x_ref = bf16[8,144,256]{2,1,0:T(8,128)(2,1)S(1)} all-to-all(bf16[8,144,256]{2,1,0:T(8,128)(2,1)S(1)} %get-tuple-element.23), channel_id=1, replica_groups={{0,2,4,6,8,10,12,14},{16,18,20,22,24,26,28,30},{32,34,36,38,40,42,44,46..., dimensions={0} | all-to-all | bytes 1179648 | tf_op jit(solution)/shard_map/all_to_all | solution.py:324
  26.7 6.5 %all-to-all-start.1 = ((bf16[8,64,128]{2,1,0:T(8,128)(2,1)}), bf16[8,64,128]{2,1,0:T(8,128)(2,1)S(1)}, u32[]{:S(2)}, u32[]{:S(2)}) async-start(bf16[8,64,128]{2,1,0:T(8,128)(2,1)} %broadcast_in_dim.6), calls=%async_computation.1 | async-start | bytes 262144 | tf_op jit(solution)/shard_map/all_to_all | solution.py:338
  33.3 1.5 %collective-permute-start = (bf16[256,128]{1,0:T(8,128)(2,1)S(1)}, bf16[256,128]{1,0:T(8,128)(2,1)S(1)}, u32[]{:S(2)}, u32[]{:S(2)}) collective-permute-start(bf16[256,128]{1,0:T(8,128)(2,1)S(1)} %bitcast.10), channel_id=1, source_target_pairs={{0,16},{2,18},{4,20},{6,22},{8,24},{10,26},{12,28},{14,30},{16,0},... | collective-permute-start | bytes 196616 | tf_op jit(solution)/shard_map/ppermute | solution.py:297
  34.8 1.9 %collective-permute-done.p16_ref = bf16[256,128]{1,0:T(8,128)(2,1)S(1)} collective-permute-done((bf16[256,128]{1,0:T(8,128)(2,1)S(1)}, bf16[256,128]{1,0:T(8,128)(2,1)S(1)}, u32[]{:S(2)}, u32[]{:S(2)}) %collective-permute-start) | collective-permute-done | bytes 65568 | tf_op jit(solution)/shard_map/ppermute | solution.py:297
  36.8 2.8 %all-to-all-done.1.c64_ref = bf16[8,64,128]{2,1,0:T(8,128)(2,1)S(1)} async-done(((bf16[8,64,128]{2,1,0:T(8,128)(2,1)}), bf16[8,64,128]{2,1,0:T(8,128)(2,1)S(1)}, u32[]{:S(2)}, u32[]{:S(2)}) %all-to-all-start.1) | async-done | bytes 131104 | tf_op jit(solution)/shard_map/all_to_all | solution.py:338
  39.6 3.9 %heads.1 = (f32[8,128,128]{2,1,0:T(8,128)S(1)}, f32[8,128,128]{2,1,0:T(8,128)S(1)}, bf16[256,128]{1,0:T(8,128)(2,1)S(1)}, bf16[8,64,128]{2,1,0:T(8,128)(2,1)}, f32[2,8,128]{2,1,0:T(8,128)S(1)}) custom-call(bf16[8,144,256]{2,1,0:T(8,128)(2,1)S(1)} %all_to_all.20.x_ref, bf16[256,128]{1,0:T(8,128)(2,1)S(1)} %collective-permute-done.p16_ref, ...), custom_call_target="tpu_custom_call" | custom-call | tf_op jit(solution)/shard_map/heads/pallas_call | solution.py:339
  43.5 2.1 %collective-permute-start.2 = (f32[1,2,8,128]{3,2,1,0:T(8,128)S(1)}, f32[1,2,8,128]{3,2,1,0:T(8,128)S(1)}, u32[]{:S(2)}, u32[]{:S(2)}) collective-permute-start(f32[1,2,8,128]{3,2,1,0:T(8,128)S(1)} %bitcast.6), channel_id=1, source_target_pairs={{0,2},{2,0},{4,6},{6,4},{8,10},{10,8},{12,14},{14,12},{16,18},{18,... | collective-permute-start | bytes 24584 | tf_op jit(solution)/shard_map/ppermute | solution.py:297
  47.7 7.8 %local.1 = (bf16[384,512]{1,0:T(8,128)(2,1)S(1)}, f32[512,512]{1,0:T(8,128)S(1)}, f32[512,512]{1,0:T(8,128)S(1)}) custom-call(bf16[512,512]{1,0:T(8,128)(2,1)S(1)} %get-tuple-element.28.q_ref, bf16[512,512]{1,0:T(8,128)(2,1)S(1)} %get-tuple-element.29.k_ref, bf16[512,512]{1,0:T(8,128)(2,1)S(1)} %get-tuple-element.30.v_ref, bf16[512,512]{1,0:T(8,128)(2,1)S(1)} %copy-done.22), custom_call_target="tpu_custom_call" | custom-call | flops 12000000000 | bytes 5000000 | tf_op jit(solution)/shard_map/local/pallas_call | solution.py:325
  58.3 3.4 %all-to-all-start.2 = ((bf16[8,64,128]{2,1,0:T(8,128)(2,1)}), bf16[8,64,128]{2,1,0:T(8,128)(2,1)S(1)}, u32[]{:S(2)}, u32[]{:S(2)}) async-start(bf16[8,64,128]{2,1,0:T(8,128)(2,1)} %get-tuple-element.27), calls=%async_computation.2 | async-start | bytes 262144 | tf_op jit(solution)/shard_map/all_to_all | solution.py:356
  61.7 1.9 %collective-permute-start.4 = (f32[4,2,8,128]{3,2,1,0:T(8,128)S(1)}, f32[4,2,8,128]{3,2,1,0:T(8,128)S(1)}, u32[]{:S(2)}, u32[]{:S(2)}) collective-permute-start(f32[4,2,8,128]{3,2,1,0:T(8,128)S(1)} %pad_maximum_fusion.1), channel_id=1, source_target_pairs={{0,8},{2,10},{4,12},{6,14},{8,0},{10,2},{12,4},{14,6},{16,24},{18,... | collective-permute-start | bytes 98312 | tf_op jit(solution)/shard_map/ppermute | solution.py:297
  63.6 1.4 %collective-permute-start.1 = (bf16[256,128]{1,0:T(8,128)(2,1)S(1)}, bf16[256,128]{1,0:T(8,128)(2,1)S(1)}, u32[]{:S(2)}, u32[]{:S(2)}) collective-permute-start(bf16[256,128]{1,0:T(8,128)(2,1)S(1)} %get-tuple-element.26), channel_id=1, source_target_pairs={{0,16},{2,18},{4,20},{6,22},{8,24},{10,26},{12,28},{14,30},{16,0},... | collective-permute-start | bytes 196616 | tf_op jit(solution)/shard_map/ppermute | solution.py:297
  65.0 1.1 collective-permute-done.4
  68.8 5.0 %all-to-all-start.3 = ((bf16[8,192,128]{2,1,0:T(8,128)(2,1)}), bf16[8,192,128]{2,1,0:T(8,128)(2,1)S(1)}, u32[]{:S(2)}, u32[]{:S(2)}) async-start(bf16[8,192,128]{2,1,0:T(8,128)(2,1)} %gather.1), calls=%async_computation.3 | async-start | bytes 786432 | tf_op jit(solution)/shard_map/all_to_all | solution.py:363
  78.8 1.2 %copy-done.25 = f32[512,512]{1,0:T(8,128)S(1)} copy-done((f32[512,512]{1,0:T(8,128)S(1)}, f32[512,512]{1,0:T(8,128)}, u32[]{:S(2)}) %copy-start.25) | copy-done | bytes 1048600
  81.1 8.2 %rest.1 = (f32[3,128,512]{2,1,0:T(8,128)S(1)}, f32[192,1024]{1,0:T(8,128)S(1)}, bf16[192,1024]{1,0:T(8,128)(2,1)}) custom-call(s32[2]{0:T(128)S(1)} %pad_add_fusion.place_ref, bf16[512,512]{1,0:T(8,128)(2,1)S(1)} %copy-done.16, bf16[512,512]{1,0:T(8,128)(2,1)S(1)} %copy-done.18, bf16[512,512]{1,0:T(8,128)(2,1)S(1)} %copy-done.20, ...), custom_call_target="tpu_custom_call" | custom-call | flops 5000000000 | bytes 9000000 | tf_op jit(solution)/shard_map/rest/pallas_call | solution.py:366
  91.0 2.5 %collective-permute-start.6 = (bf16[192,1024]{1,0:T(8,128)(2,1)}, bf16[192,1024]{1,0:T(8,128)(2,1)}, u32[]{:S(2)}, u32[]{:S(2)}) collective-permute-start(bf16[192,1024]{1,0:T(8,128)(2,1)} %get-tuple-element.40), channel_id=1, source_target_pairs={{0,1},{1,0},{2,3},{3,2},{4,5},{5,4},{6,7},{7,6},{8,9},{9,8},{10,11... | collective-permute-start | bytes 1179656 | tf_op jit(solution)/shard_map/ppermute | solution.py:297
  93.5 1.1 %copy-done.4 = f32[3,128,512]{2,1,0:T(8,128)S(1)} copy-done((f32[3,128,512]{2,1,0:T(8,128)S(1)}, f32[3,128,512]{2,1,0:T(8,128)}, u32[]{:S(2)}) %copy-start.4) | copy-done | bytes 786456
  95.4 2.0 %dil.1 = (f32[64,1024]{1,0:T(8,128)S(1)}, bf16[64,1024]{1,0:T(8,128)(2,1)S(1)}) custom-call(s32[2]{0:T(128)S(1)} %pad_add_fusion.place_ref, bf16[128,128]{1,0:T(8,128)(2,1)S(1)} %copy-done.14, bf16[8,192,128]{2,1,0:T(8,128)(2,1)S(1)} %all-to-all-done.3.got_ref, f32[3,128,512]{2,1,0:T(8,128)S(1)} %copy-done.4, bf16[1024,512]{1,0:T(8,128)(2,1)S(1)} %copy-done, ...), custom_call_target="tpu_custom_call" | custom-call | tf_op jit(solution)/shard_map/dil/pallas_call | solution.py:383
  98.0 5.5 %collective-permute-done.6.got_r = bf16[192,1024]{1,0:T(8,128)(2,1)} collective-permute-done((bf16[192,1024]{1,0:T(8,128)(2,1)}, bf16[192,1024]{1,0:T(8,128)(2,1)}, u32[]{:S(2)}, u32[]{:S(2)}) %collective-permute-start.6) | collective-permute-done | bytes 393248 | tf_op jit(solution)/shard_map/ppermute | solution.py:297
  103.5 2.7 %collective-permute-done.5.got_d = bf16[64,1024]{1,0:T(8,128)(2,1)S(1)} collective-permute-done((bf16[64,1024]{1,0:T(8,128)(2,1)S(1)}, bf16[64,1024]{1,0:T(8,128)(2,1)S(1)}, u32[]{:S(2)}, u32[]{:S(2)}) %collective-permute-start.5) | collective-permute-done | bytes 131104 | tf_op jit(solution)/shard_map/ppermute | solution.py:297
  106.2 2.1 %last.1 = bf16[256,1024]{1,0:T(8,128)(2,1)} custom-call(bf16[256,256]{1,0:T(8,128)(2,1)S(1)} %copy-done.12, f32[64,1024]{1,0:T(8,128)S(1)} %get-tuple-element.37.keep_d, bf16[64,1024]{1,0:T(8,128)(2,1)S(1)} %collective-permute-done.5.got_d, f32[192,1024]{1,0:T(8,128)S(1)} %copy-done.6, bf16[192,1024]{1,0:T(8,128)(2,1)} %collective-permute-done.6.got_r), custom_call_target="tpu_custom_call" | custom-call | tf_op jit(solution)/shard_map/last/pallas_call | solution.py:392
  (69 shorter events, 21.5 us)
Async XLA Ops:
  0.0 1.0 copy-start.7
  1.0 1.0 copy-start.8
  2.1 1.0 copy-start.9
  9.9 36.7 %copy-start.15 = (bf16[512,512]{1,0:T(8,128)(2,1)}, bf16[512,512]{1,0:T(8,128)(2,1)S(1)}, u32[]{:S(2)}) copy-start(bf16[512,512]{1,0:T(8,128)(2,1)S(1)} %get-tuple-element.28.q_ref) | copy-start | bytes 1572868
  9.9 36.7 %copy-start.17 = (bf16[512,512]{1,0:T(8,128)(2,1)}, bf16[512,512]{1,0:T(8,128)(2,1)S(1)}, u32[]{:S(2)}) copy-start(bf16[512,512]{1,0:T(8,128)(2,1)S(1)} %get-tuple-element.29.k_ref) | copy-start | bytes 1572868
  9.9 36.7 %copy-start.19 = (bf16[512,512]{1,0:T(8,128)(2,1)}, bf16[512,512]{1,0:T(8,128)(2,1)S(1)}, u32[]{:S(2)}) copy-start(bf16[512,512]{1,0:T(8,128)(2,1)S(1)} %get-tuple-element.30.v_ref) | copy-start | bytes 1572868
  26.7 12.8 %all-to-all-start.1 = ((bf16[8,64,128]{2,1,0:T(8,128)(2,1)}), bf16[8,64,128]{2,1,0:T(8,128)(2,1)S(1)}, u32[]{:S(2)}, u32[]{:S(2)}) async-start(bf16[8,64,128]{2,1,0:T(8,128)(2,1)} %broadcast_in_dim.6), calls=%async_computation.1 | async-start | bytes 262144 | tf_op jit(solution)/shard_map/all_to_all | solution.py:338
  33.3 3.5 %collective-permute-start = (bf16[256,128]{1,0:T(8,128)(2,1)S(1)}, bf16[256,128]{1,0:T(8,128)(2,1)S(1)}, u32[]{:S(2)}, u32[]{:S(2)}) collective-permute-start(bf16[256,128]{1,0:T(8,128)(2,1)S(1)} %bitcast.10), channel_id=1, source_target_pairs={{0,16},{2,18},{4,20},{6,22},{8,24},{10,26},{12,28},{14,30},{16,0},... | collective-permute-start | bytes 196616 | tf_op jit(solution)/shard_map/ppermute | solution.py:297
  43.5 2.9 %collective-permute-start.2 = (f32[1,2,8,128]{3,2,1,0:T(8,128)S(1)}, f32[1,2,8,128]{3,2,1,0:T(8,128)S(1)}, u32[]{:S(2)}, u32[]{:S(2)}) collective-permute-start(f32[1,2,8,128]{3,2,1,0:T(8,128)S(1)} %bitcast.6), channel_id=1, source_target_pairs={{0,2},{2,0},{4,6},{6,4},{8,10},{10,8},{12,14},{14,12},{16,18},{18,... | collective-permute-start | bytes 24584 | tf_op jit(solution)/shard_map/ppermute | solution.py:297
  46.4 15.3 %collective-permute-start.3 = (f32[2,2,8,128]{3,2,1,0:T(8,128)S(1)}, f32[2,2,8,128]{3,2,1,0:T(8,128)S(1)}, u32[]{:S(2)}, u32[]{:S(2)}) collective-permute-start(f32[2,2,8,128]{3,2,1,0:T(8,128)S(1)} %pad_maximum_fusion.2), channel_id=1, source_target_pairs={{0,4},{2,6},{4,0},{6,2},{8,12},{10,14},{12,8},{14,10},{16,20},{18,... | collective-permute-start | bytes 49160 | tf_op jit(solution)/shard_map/ppermute | solution.py:297
  46.7 1.0 copy-start.22
  58.3 9.6 %all-to-all-start.2 = ((bf16[8,64,128]{2,1,0:T(8,128)(2,1)}), bf16[8,64,128]{2,1,0:T(8,128)(2,1)S(1)}, u32[]{:S(2)}, u32[]{:S(2)}) async-start(bf16[8,64,128]{2,1,0:T(8,128)(2,1)} %get-tuple-element.27), calls=%async_computation.2 | async-start | bytes 262144 | tf_op jit(solution)/shard_map/all_to_all | solution.py:356
  61.7 4.4 %collective-permute-start.4 = (f32[4,2,8,128]{3,2,1,0:T(8,128)S(1)}, f32[4,2,8,128]{3,2,1,0:T(8,128)S(1)}, u32[]{:S(2)}, u32[]{:S(2)}) collective-permute-start(f32[4,2,8,128]{3,2,1,0:T(8,128)S(1)} %pad_maximum_fusion.1), channel_id=1, source_target_pairs={{0,8},{2,10},{4,12},{6,14},{8,0},{10,2},{12,4},{14,6},{16,24},{18,... | collective-permute-start | bytes 98312 | tf_op jit(solution)/shard_map/ppermute | solution.py:297
  63.6 3.7 %collective-permute-start.1 = (bf16[256,128]{1,0:T(8,128)(2,1)S(1)}, bf16[256,128]{1,0:T(8,128)(2,1)S(1)}, u32[]{:S(2)}, u32[]{:S(2)}) collective-permute-start(bf16[256,128]{1,0:T(8,128)(2,1)S(1)} %get-tuple-element.26), channel_id=1, source_target_pairs={{0,16},{2,18},{4,20},{6,22},{8,24},{10,26},{12,28},{14,30},{16,0},... | collective-permute-start | bytes 196616 | tf_op jit(solution)/shard_map/ppermute | solution.py:297
  68.8 24.7 %all-to-all-start.3 = ((bf16[8,192,128]{2,1,0:T(8,128)(2,1)}), bf16[8,192,128]{2,1,0:T(8,128)(2,1)S(1)}, u32[]{:S(2)}, u32[]{:S(2)}) async-start(bf16[8,192,128]{2,1,0:T(8,128)(2,1)} %gather.1), calls=%async_computation.3 | async-start | bytes 786432 | tf_op jit(solution)/shard_map/all_to_all | solution.py:363
  78.8 1.2 %copy-start.25 = (f32[512,512]{1,0:T(8,128)S(1)}, f32[512,512]{1,0:T(8,128)}, u32[]{:S(2)}) copy-start(f32[512,512]{1,0:T(8,128)} %copy-done.24) | copy-start | bytes 3145732
  81.1 12.4 %copy-start = (bf16[1024,512]{1,0:T(8,128)(2,1)S(1)}, bf16[1024,512]{1,0:T(8,128)(2,1)}, u32[]{:S(2)}) copy-start(bf16[1024,512]{1,0:T(8,128)(2,1)} %wq_ref.3) | copy-start | bytes 3145732
  81.1 12.4 %copy-start.1 = (bf16[1024,512]{1,0:T(8,128)(2,1)S(1)}, bf16[1024,512]{1,0:T(8,128)(2,1)}, u32[]{:S(2)}) copy-start(bf16[1024,512]{1,0:T(8,128)(2,1)} %wk_ref.3) | copy-start | bytes 3145732
  81.1 12.4 %copy-start.2 = (bf16[1024,512]{1,0:T(8,128)(2,1)S(1)}, bf16[1024,512]{1,0:T(8,128)(2,1)}, u32[]{:S(2)}) copy-start(bf16[1024,512]{1,0:T(8,128)(2,1)} %wv_ref.3) | copy-start | bytes 3145732
  91.0 12.5 %collective-permute-start.6 = (bf16[192,1024]{1,0:T(8,128)(2,1)}, bf16[192,1024]{1,0:T(8,128)(2,1)}, u32[]{:S(2)}, u32[]{:S(2)}) collective-permute-start(bf16[192,1024]{1,0:T(8,128)(2,1)} %get-tuple-element.40), channel_id=1, source_target_pairs={{0,1},{1,0},{2,3},{3,2},{4,5},{5,4},{6,7},{7,6},{8,9},{9,8},{10,11... | collective-permute-start | bytes 1179656 | tf_op jit(solution)/shard_map/ppermute | solution.py:297
  93.5 1.1 %copy-start.4 = (f32[3,128,512]{2,1,0:T(8,128)S(1)}, f32[3,128,512]{2,1,0:T(8,128)}, u32[]{:S(2)}) copy-start(f32[3,128,512]{2,1,0:T(8,128)} %copy-done.3) | copy-start | bytes 2359300
  95.4 10.8 %copy-start.6 = (f32[192,1024]{1,0:T(8,128)S(1)}, f32[192,1024]{1,0:T(8,128)}, u32[]{:S(2)}) copy-start(f32[192,1024]{1,0:T(8,128)} %copy-done.5) | copy-start | bytes 2359300
  95.4 10.8 %copy-start.12 = (bf16[256,256]{1,0:T(8,128)(2,1)S(1)}, bf16[256,256]{1,0:T(8,128)(2,1)}, u32[]{:S(2)}) copy-start(bf16[256,256]{1,0:T(8,128)(2,1)} %constant.21.clone.perm_ref) | copy-start | bytes 393220
  97.4 8.8 %collective-permute-start.5 = (bf16[64,1024]{1,0:T(8,128)(2,1)S(1)}, bf16[64,1024]{1,0:T(8,128)(2,1)S(1)}, u32[]{:S(2)}, u32[]{:S(2)}) collective-permute-start(bf16[64,1024]{1,0:T(8,128)(2,1)S(1)} %get-tuple-element.38), channel_id=1, source_target_pairs={{0,1},{1,0},{2,3},{3,2},{4,5},{5,4},{6,7},{7,6},{8,9},{9,8},{10,11... | collective-permute-start | bytes 393224 | tf_op jit(solution)/shard_map/ppermute | solution.py:297
  (15 other events, 14.2 us)

commit v2 on v1

v2 whole, which is shorter than its diff:
```python
import functools

import jax
import jax.numpy as jnp
import numpy as np
from jax import lax
from jax.experimental import pallas as pl
from jax.experimental.pallas import tpu as pltpu
from jax.sharding import PartitionSpec as P

BF16 = jnp.bfloat16
F32 = jnp.float32
ROWS = 512
DIL = 128
REST = ROWS - DIL
LANES = 128
HEADS = 8
STAT_ROWS = 16
MIB = 1024 * 1024
LARGE = 62 * MIB
TALL = 20 * 1024
LOW = -1e30


def frame_order():
    r = np.arange(DIL)
    dil = np.concatenate([r[r % 16 == 0], r[(r % 4 == 0) & (r % 16 != 0)], r[r % 4 != 0]])
    f = np.arange(ROWS)
    return dil, np.concatenate([dil * 4, f[f % 4 != 0]])


def one_hot(index, width):
    out = np.zeros((len(index), width), np.float32)
    out[np.arange(len(index)), index] = 1
    return out


def order_hot():
    p = lax.broadcasted_iota(jnp.int32, (ROWS, LANES), 0)

    def skip(i):
        return i + lax.shift_right_logical(i * 171, 9) + 1

    frame = jnp.where(
        p < 8,
        64 * p,
        jnp.where(p < 32, 16 * skip(p - 8), jnp.where(p < DIL, 4 * skip(p - 32), skip(p - DIL))),
    )
    lane = lax.broadcasted_iota(jnp.int32, (ROWS, LANES), 1)
    return jnp.concatenate(
        [jnp.where(frame == lane + i * LANES, 1.0, 0.0).astype(BF16) for i in range(ROWS // LANES)], axis=1
    )


def dot_tt(a, b):
    return lax.dot_general(a, b, (((1,), (1,)), ((), ())), preferred_element_type=F32)


def dot(a, b):
    return jnp.dot(a, b, preferred_element_type=F32)


def half_mask(side):
    lane = lax.broadcasted_iota(jnp.int32, (1, LANES), 1)
    return jnp.where((lane >= 64) == (side == 1), 1.0, 0.0)


def pair(x):
    return jnp.concatenate([x * half_mask(0).astype(BF16), x * half_mask(1).astype(BF16)], axis=0)


def choose(first, second):
    lane = lax.broadcasted_iota(jnp.int32, first.shape, 1)
    return jnp.where(lane < 64, first, second)


def stats(scores, grad_prob):
    top = jnp.max(scores, axis=0, keepdims=True)
    e = jnp.exp(scores - top)
    total = jnp.sum(e, axis=0, keepdims=True)
    delta = jnp.sum(e * grad_prob, axis=0, keepdims=True) / total
    return e, total, top + jnp.log(total), delta


def thirds(x):
    a = x.astype(BF16).astype(F32)
    b = (x - a).astype(BF16).astype(F32)
    return [a, b, x - a - b]


def pack_kernel(perm_hbm, q_hbm, k_hbm, v_hbm, g_hbm, x_hbm, perm_ref, in_ref, x_ref, sems, out_sems, perm_sem):
    def fetch(s, i):
        cols = pl.ds(s * LANES, LANES)
        source = (q_hbm, k_hbm, v_hbm, g_hbm)[i]
        return pltpu.make_async_copy(source.at[:, cols], in_ref.at[s, i], sems.at[s, i])

    def put(s):
        return pltpu.make_async_copy(x_ref.at[pl.ds(2 * s, 2)], x_hbm.at[pl.ds(2 * s, 2)], out_sems.at[s])

    perm_copy = pltpu.make_async_copy(perm_hbm, perm_ref, perm_sem)
    perm_copy.start()
    for s in range(4):
        for i in range(4):
            fetch(s, i).start()
    perm_copy.wait()
    for s in range(4):
        for i in range(4):
            fetch(s, i).wait()
        k, v = in_ref[s, 1], in_ref[s, 2]
        block = jnp.concatenate([in_ref[s, 0] * BF16(0.125), k, v, in_ref[s, 3]], axis=1)
        block = dot(perm_ref[...], block).astype(BF16)
        qd, kd, vd, gd = (block[:, i * LANES : (i + 1) * LANES] for i in range(4))
        scores = dot_tt(k, pair(qd))
        grad_prob = dot_tt(v, pair(gd))
        _, _, lse, delta = stats(scores, grad_prob)
        for h in range(2):
            part = slice(h * DIL, (h + 1) * DIL)
            rows = thirds(lse[:, part]) + thirds(delta[:, part])
            rows = jnp.concatenate(rows + [jnp.zeros((STAT_ROWS - 6, LANES), F32)], axis=0)
            cols = slice(h * 64, h * 64 + 64)
            x_ref[2 * s + h, :DIL, :] = jnp.concatenate([kd[:, cols], vd[:, cols], qd[:, cols], gd[:, cols]], axis=1)
            x_ref[2 * s + h, DIL:, :] = jnp.concatenate([rows, jnp.zeros_like(rows)], axis=1).astype(BF16)
        put(s).start()
    for s in range(4):
        put(s).wait()


def local_kernel(perm_ref, q_ref, k_ref, v_ref, g_ref, in_ref, dq_ref, sum_ref, token_ref):
    token_ref[...] = jnp.zeros_like(token_ref)
    block = jnp.concatenate([q_ref[...] * BF16(0.125), g_ref[...]], axis=1)
    block = dot(perm_ref[...], block).astype(BF16)
    in_ref[0] = block[:DIL, :LANES]
    in_ref[1] = block[:DIL, LANES:]
    q, g = block[DIL:, :LANES], block[DIL:, LANES:]
    k, v = k_ref[...], v_ref[...]
    q2, g2 = pair(q), pair(g)
    scores = dot_tt(k, q2)
    grad_prob = dot_tt(v, g2)
    e, total, _, delta = stats(scores, grad_prob)
    p = e * (1.0 / total)
    ds = (p * (grad_prob - delta)).astype(BF16)
    dq = dot((k * BF16(0.125)).T, ds)
    dq_ref[...] = jnp.concatenate([dq[:64, :REST], dq[64:, REST:]], axis=0).T.astype(BF16)
    sum_ref[0] = dot(ds, q2).astype(BF16)
    sum_ref[1] = dot(p.astype(BF16), g2).astype(BF16)


def pick16_kernel(x_ref, _, b16_ref):
    b16_ref[...] = x_ref[:, :32, :LANES].reshape(256, LANES)


def pick64_kernel(b16_ref, b64_ref):
    rows = b16_ref[...].reshape(HEADS, 32, LANES)[:, :16].astype(F32)[:, :8].reshape(64, LANES).astype(BF16)
    for a in range(HEADS):
        b64_ref[a] = rows


def head_kernel(x_ref, p16_ref, c64_ref, own_ref, dq_ref, part16_ref, part64_ref, stat_ref):
    def products(kv, qg):
        both = dot_tt(kv, pair(qg))
        return both[:, : qg.shape[0]], both[:, qg.shape[0] :]

    def grads(kv, qg, scores, grad_prob, lse, delta):
        p = jnp.exp(scores - lse)
        ds = (p * (grad_prob - delta)).astype(BF16)
        dkv = dot(jnp.concatenate([ds, p.astype(BF16)], axis=1), pair(qg))
        dq = dot((kv * BF16(0.125)).T, ds).T
        return dkv, dq

    def spread(row, width, fill):
        lines = []
        for s in range(HEADS):
            piece = row[:, s * width : (s + 1) * width]
            if width < DIL:
                piece = jnp.concatenate([piece, jnp.full((1, DIL - width), fill, F32)], axis=1)
            lines.append(piece)
        return jnp.concatenate(lines, axis=0)

    def collect(table, width):
        return jnp.concatenate([table[s : s + 1, :width] for s in range(HEADS)], axis=1)

    segments = []
    for s in range(2):
        block = x_ref[4 * s : 4 * s + 4, :DIL, :].reshape(4 * DIL, 2 * LANES)
        segments.append((block[:, :LANES], block[:, LANES:]))
    block16 = x_ref[:, :32, :].reshape(256, 2 * LANES)
    kv16 = jnp.concatenate([block16[:, :LANES], p16_ref[...]], axis=0)
    qg16 = block16[:, LANES:]
    qg64 = x_ref[:, :16, LANES:].astype(F32)[:, :8, :].reshape(64, LANES).astype(BF16)
    kv64 = c64_ref[...].reshape(512, LANES)

    lse1, delta1 = [], []
    for s in range(HEADS):
        rows = x_ref[s, DIL:, :LANES].astype(F32)
        lse1.append(rows[0:1] + rows[1:2] + rows[2:3])
        delta1.append(rows[3:4] + rows[4:5] + rows[5:6])
    lses = [jnp.concatenate(lse1, axis=0)]
    deltas = [jnp.concatenate(delta1, axis=0)]

    made = [products(kv, qg) for kv, qg in segments]
    got = [stats(*pair) for pair in made]
    lses.append(spread(jnp.concatenate([got[0][2], got[1][2]], axis=1), DIL, LOW))
    deltas.append(spread(jnp.concatenate([got[0][3], got[1][3]], axis=1), DIL, 0.0))
    made16 = products(kv16, qg16)
    got = stats(*made16)
    lses.append(spread(got[2], 32, LOW))
    deltas.append(spread(got[3], 32, 0.0))
    made64 = products(kv64, qg64)
    got = stats(*made64)
    lses.append(spread(got[2], 8, LOW))
    deltas.append(spread(got[3], 8, 0.0))

    top = functools.reduce(jnp.maximum, lses)
    parts = [jnp.exp(x - top) for x in lses]
    total = sum(parts)
    lse = top + jnp.log(total)
    delta = sum(w * d for w, d in zip(parts, deltas)) / total
    stat_ref[0] = lse
    stat_ref[1] = delta

    for s in range(2):
        row = [jnp.concatenate([t[4 * s + i : 4 * s + i + 1] for i in range(4)], axis=1) for t in (lse, delta)]
        dkv, dq = grads(*segments[s], *made[s], *row)
        own_ref[4 * s : 4 * s + 4] = dkv.reshape(4, DIL, LANES)
        dq_ref[4 * s : 4 * s + 4] = dq.reshape(4, DIL, LANES)
    dkv, dq = grads(kv16, qg16, *made16, collect(lse, 32), collect(delta, 32))
    own_ref[:, :32, :] = own_ref[:, :32, :] + dkv[:256].reshape(HEADS, 32, LANES)
    part16_ref[...] = dkv[256:].astype(BF16)
    dq_ref[:, :32, :] = dq_ref[:, :32, :] + dq.reshape(HEADS, 32, LANES)
    dkv, dq = grads(kv64, qg64, *made64, collect(lse, 8), collect(delta, 8))
    part64_ref[...] = dkv.reshape(HEADS, 64, LANES).astype(BF16)
    dq_ref[:, :8, :] = dq_ref[:, :8, :] + dq.reshape(HEADS, 8, LANES)


def gather_kernel(own_ref, dq_ref, got16_ref, got64_ref, out_ref):
    got16 = got16_ref[...].astype(F32).reshape(HEADS, 32, LANES)
    got64 = got64_ref[...].astype(F32)
    got64 = sum(got64[i] for i in range(HEADS)).reshape(HEADS, 8, LANES)
    first = got16[:, :8] + got64
    dkv = own_ref[...]
    dkv = jnp.concatenate([dkv[:, :8] + first, dkv[:, 8:32] + got16[:, 8:], dkv[:, 32:]], axis=1)
    out_ref[:, :DIL, :] = dkv.astype(BF16)
    for s in range(HEADS):
        dq = dq_ref[s]
        out_ref[s, DIL:, :] = jnp.concatenate([dq[:64, :64], dq[64:, :64]], axis=1).astype(BF16)


def rest_kernel(
    st_hbm, in_hbm, k_hbm, v_hbm, sum_hbm, dq_hbm, wq_hbm, wk_hbm, wv_hbm,
    dil_ref, keep_ref, send_ref, w_hbm,
    st_ref, in_ref, k_ref, v_ref, sum_ref, dq_s, w_s, dk_s, dv_s, sems, out_sems,
):
    pairs = [(st_hbm, st_ref), (in_hbm, in_ref), (k_hbm, k_ref), (v_hbm, v_ref), (sum_hbm, sum_ref)]
    pairs += [(dq_hbm, dq_s)]
    pairs += [(w, w_s.at[i]) for i, w in enumerate((wq_hbm, wk_hbm, wv_hbm))]
    fetches = [pltpu.make_async_copy(a, b, sems.at[i]) for i, (a, b) in enumerate(pairs)]
    for fetch in fetches:
        fetch.start()
    line = lax.rem(lax.axis_index("tm"), 8)
    head = lax.axis_index("head")
    perm = order_hot()
    for fetch in fetches[:4]:
        fetch.wait()
    for slab in range(4):
        cols = slice(slab * LANES, (slab + 1) * LANES)
        k, v = k_ref[:, cols], v_ref[:, cols]
        q2, g2 = pair(in_ref[0, :, cols]), pair(in_ref[1, :, cols])
        scores = dot_tt(k, q2)
        grad_prob = dot_tt(v, g2)
        lse, delta = [], []
        for h in range(2):
            at = jnp.bitwise_xor(2 * slab + h, line)
            lse.append(st_ref[at, 0, pl.ds(line, 1), :])
            delta.append(st_ref[at, 1, pl.ds(line, 1), :])
        p = jnp.exp(scores - jnp.concatenate(lse, axis=1))
        ds = (p * (grad_prob - jnp.concatenate(delta, axis=1))).astype(BF16)
        dq = dot((k * BF16(0.125)).T, ds)
        dil_ref[0, :, cols] = jnp.concatenate([dq[:64, :DIL], dq[64:, DIL:]], axis=0).T.astype(BF16)
        dk, dv = dot(ds, q2), dot(p.astype(BF16), g2)
        if slab == 0:
            fetches[4].wait()
        dkv = [dk + sum_ref[0, :, cols].astype(F32), dv + sum_ref[1, :, cols].astype(F32)]
        moved = dot(perm, jnp.concatenate(dkv, axis=1).astype(BF16)).astype(BF16)
        dil_ref[1, :, cols] = moved[:DIL, :LANES]
        dil_ref[2, :, cols] = moved[:DIL, LANES:]
        dk_s[:, cols] = moved[DIL:, :LANES]
        dv_s[:, cols] = moved[DIL:, LANES:]
    for fetch in fetches[5:]:
        fetch.wait()
    puts = [pltpu.make_async_copy(w_s.at[i], w_hbm.at[i, pl.ds(0, 1024)], out_sems.at[i]) for i in range(3)]
    for put in puts:
        put.start()
    half = REST // 2
    keep = pl.ds(pl.multiple_of(head * half, half), half)
    send = pl.ds(pl.multiple_of((1 - head) * half, half), half)
    for i, grad in enumerate((dq_s, dk_s, dv_s)):
        keep_ref[i] = grad[keep, :]
    out = dot_tt(dq_s[send, :], w_s[0]) + dot_tt(dk_s[send, :], w_s[1]) + dot_tt(dv_s[send, :], w_s[2])
    send_ref[...] = out.astype(BF16)
    for put in puts:
        put.wait()


def dil_kernel(perm_ref, got_ref, dil_ref, kept_ref, w_hbm, keep_ref, send_ref, keep_r, out_s, w_s, sems):
    head = lax.axis_index("head")
    fetches = [pltpu.make_async_copy(w_hbm.at[i, pl.ds(0, 1024)], w_s.at[i], sems.at[i]) for i in range(3)]
    for fetch in fetches:
        fetch.start()

    def both(pieces):
        return jnp.concatenate(pieces, axis=1)

    dk = both([got_ref[h, :DIL, :64].astype(F32) for h in range(HEADS)])
    dv = both([got_ref[h, :DIL, 64:].astype(F32) for h in range(HEADS)])
    dq = jnp.concatenate(
        [both([got_ref[h, DIL:, s * 64 : s * 64 + 64].astype(F32) for h in range(HEADS)]) for s in range(2)], axis=0
    )
    perm = perm_ref[...]
    grads = [dot(perm, (grad + dil_ref[i].astype(F32)).astype(BF16)).astype(BF16) for i, grad in enumerate((dq, dk, dv))]
    out = None
    for i, rows in enumerate(grads):
        fetches[i].wait()
        part = dot_tt(jnp.concatenate([rows, kept_ref[i]], axis=0), w_s[i])
        out = part if out is None else out + part
    out_s[...] = out[:DIL]
    keep_r[...] = out[DIL:].astype(BF16)
    half = DIL // 2
    keep_ref[...] = out_s[pl.ds(pl.multiple_of(head * half, half), half), :]
    send_ref[...] = out_s[pl.ds(pl.multiple_of((1 - head) * half, half), half), :].astype(BF16)


def last_kernel(perm_ref, keep_d, got_d, keep_r, got_r, out_ref):
    rows = jnp.concatenate(
        [keep_d[...] + got_d[...].astype(F32), keep_r[...].astype(F32) + got_r[...].astype(F32)], axis=0
    ).astype(BF16)
    out_ref[...] = dot(perm_ref[...], rows).astype(BF16)


def params(limit=LARGE):
    return pltpu.CompilerParams(vmem_limit_bytes=limit)


def cost(flops, bytes_accessed, exps):
    return pl.CostEstimate(flops=flops, bytes_accessed=bytes_accessed, transcendentals=exps)


def shape(dims, dtype):
    return jax.ShapeDtypeStruct(dims, dtype)


def slab_spec(rows):
    return pl.BlockSpec((rows, LANES), lambda s: (0, s))


def whole(dims):
    return pl.BlockSpec(dims, lambda s: (0,) * len(dims))


def swap(x, axis, bits):
    return lax.ppermute(x, axis, [(i, i ^ bits) for i in range(lax.axis_size(axis))])


def on_device(queries, keys, values, grad_attn, w_query, w_key, w_value):
    size = lax.axis_size("tm")
    lines = [[a * 8 + j for j in range(8)] for a in range(size // 8)]
    across = [[b * 64 + a * 8 + j for a in range(8)] for b in range(size // 64) for j in range(8)]
    hbm = pl.BlockSpec(memory_space=pltpu.HBM)
    dil, order = frame_order()
    perm = jnp.asarray(one_hot(order, ROWS), BF16)
    perm_first = jnp.asarray(one_hot(order[:DIL], ROWS), BF16)
    perm_dil = jnp.asarray(one_hot(np.argsort(dil), DIL), BF16)
    f = np.arange(256)
    seat = np.where(f % 4 == 0, f // 4, 64 + f - f // 4 - 1)
    perm_last = jnp.asarray(one_hot(seat, 256), BF16)

    sent = pl.pallas_call(
        pack_kernel,
        in_specs=[hbm] * 5,
        out_specs=hbm,
        out_shape=shape((HEADS, DIL + STAT_ROWS, 256), BF16),
        scratch_shapes=[
            pltpu.VMEM((DIL, ROWS), BF16),
            pltpu.VMEM((4, 4, ROWS, LANES), BF16),
            pltpu.VMEM((HEADS, DIL + STAT_ROWS, 256), BF16),
            pltpu.SemaphoreType.DMA((4, 4)),
            pltpu.SemaphoreType.DMA((4,)),
            pltpu.SemaphoreType.DMA,
        ],
        compiler_params=params(),
        name="pack",
    )(perm_first, queries, keys, values, grad_attn)

    x = lax.all_to_all(sent, "tm", 0, 0, axis_index_groups=lines, tiled=True)

    def stack_spec(planes, rows):
        return pl.BlockSpec((planes, rows, LANES), lambda s: (0, 0, s))

    ins, dq1, sums, token = pl.pallas_call(
        local_kernel,
        grid=(4,),
        in_specs=[whole((ROWS, ROWS))] + [slab_spec(ROWS)] * 4,
        out_specs=[stack_spec(2, DIL), slab_spec(REST), stack_spec(2, ROWS), whole((8, LANES))],
        out_shape=[
            shape((2, DIL, 512), BF16),
            shape((REST, 512), BF16),
            shape((2, ROWS, 512), BF16),
            shape((8, LANES), F32),
        ],
        compiler_params=params(),
        cost_estimate=cost(12_000_000_000, 5_000_000, 1_600_000),
        name="local",
    )(perm, queries, keys, values, grad_attn)

    mine16 = pl.pallas_call(
        pick16_kernel, out_shape=shape((256, LANES), BF16), compiler_params=params(8 * MIB), name="pick16"
    )(x, token)
    p16 = swap(mine16, "tm", 8)
    mine64 = pl.pallas_call(
        pick64_kernel, out_shape=shape((8, 64, LANES), BF16), compiler_params=params(8 * MIB), name="pick64"
    )(mine16)
    c64 = lax.all_to_all(mine64, "tm", 0, 0, axis_index_groups=across, tiled=True)
    own, dq_own, part16, part64, stat = pl.pallas_call(
        head_kernel,
        out_shape=[
            shape((HEADS, DIL, LANES), F32),
            shape((HEADS, DIL, LANES), F32),
            shape((256, LANES), BF16),
            shape((8, 64, LANES), BF16),
            shape((2, HEADS, DIL), F32),
        ],
        compiler_params=params(24 * MIB),
        name="heads",
    )(x, p16, c64)

    st = stat[None]
    for bit in (1, 2, 4):
        st = jnp.concatenate([st, swap(st, "tm", bit)], axis=0)
    got16 = swap(part16, "tm", 8)
    got64 = lax.all_to_all(part64, "tm", 0, 0, axis_index_groups=across, tiled=True)
    back = pl.pallas_call(
        gather_kernel,
        out_shape=shape((HEADS, DIL + 64, LANES), BF16),
        compiler_params=params(8 * MIB),
        name="gather",
    )(own, dq_own, got16, got64)
    got = lax.all_to_all(back, "tm", 0, 0, axis_index_groups=lines, tiled=True)

    vmem = pl.BlockSpec(memory_space=pltpu.VMEM)
    half = REST // 2
    dil_own, kept, send_r, weights = pl.pallas_call(
        rest_kernel,
        in_specs=[hbm] * 9,
        out_specs=[pl.BlockSpec(memory_space=pltpu.VMEM)] * 3 + [hbm],
        out_shape=[
            shape((3, DIL, 512), BF16),
            shape((3, half, 512), BF16),
            shape((half, 1024), BF16),
            shape((3, TALL, 512), BF16),
        ],
        scratch_shapes=[
            pltpu.VMEM((8, 2, HEADS, DIL), F32),
            pltpu.VMEM((2, DIL, 512), BF16),
            pltpu.VMEM((ROWS, 512), BF16),
            pltpu.VMEM((ROWS, 512), BF16),
            pltpu.VMEM((2, ROWS, 512), BF16),
            pltpu.VMEM((REST, 512), BF16),
            pltpu.VMEM((3, 1024, 512), BF16),
            pltpu.VMEM((REST, 512), BF16),
            pltpu.VMEM((REST, 512), BF16),
            pltpu.SemaphoreType.DMA((9,)),
            pltpu.SemaphoreType.DMA((3,)),
        ],
        compiler_params=params(),
        cost_estimate=cost(5_000_000_000, 9_000_000, 600_000),
        name="rest",
    )(st, ins, keys, values, sums, dq1, w_query, w_key, w_value)
    got_r = swap(send_r, "head", 1)

    keep_d, send_d, keep_r = pl.pallas_call(
        dil_kernel,
        in_specs=[vmem] * 4 + [hbm],
        out_shape=[shape((DIL // 2, 1024), F32), shape((DIL // 2, 1024), BF16), shape((half, 1024), BF16)],
        scratch_shapes=[
            pltpu.VMEM((DIL, 1024), F32),
            pltpu.VMEM((3, 1024, 512), BF16),
            pltpu.SemaphoreType.DMA((3,)),
        ],
        compiler_params=params(12 * MIB),
        name="dil",
    )(perm_dil, got, dil_own, kept, weights)
    got_d = swap(send_d, "head", 1)
    return pl.pallas_call(
        last_kernel,
        out_shape=shape((256, 1024), BF16),
        compiler_params=params(8 * MIB),
        name="last",
    )(perm_last, keep_d, got_d, keep_r, got_r)


def solution(mesh):
    return jax.shard_map(
        on_device,
        mesh=mesh,
        in_specs=(
            P("tm", "head"),
            P("tm", "head"),
            P("tm", "head"),
            P("tm", "head"),
            P(None, "head"),
            P(None, "head"),
            P(None, "head"),
        ),
        out_specs=P(("tm", "head"), None),
        check_vma=False,
    )
```

time: 110 us -> 83.3 us (0.76)
  local copies, waits for them, and re-layouts: 21.4 us -> 2.74 us
  blocking collectives: 16.1 us -> 0 us
  starting transfers between devices: 25.1 us -> 33.2 us
  Pallas kernels: 28.8 us -> 31.6 us
  waiting for transfers between devices: 16.1 us -> 14.5 us
    unnamed x58 -> x10, local copies, waits for them, and re-layouts: 20.7 us -> 2.74 us
    all_to_all x1 -> x0, blocking collectives: 16.1 us -> none  [on_device(): x = lax.all_to_all(sent, 'tm', 0, 0, axis_index_groups=lines, tiled=True)]
    all_to_all x1 -> x2, starting transfers between devices: 6.55 us -> 12.5 us  [the longest x1 6.69 us: on_device(): x = lax.all_to_all(sent, 'tm', 0, 0, axis_index_groups=lines, tiled=True)]
    pallas_call x4 -> x6, Pallas kernels: 21.9 us -> 26.1 us  [the longest x1 10 us: on_device(): pl.pallas_call(local_kernel, grid=(4,), in_specs=[whole((ROWS, ROWS))] +...]
    ppermute x7, starting transfers between devices: 10.2 us -> 11.6 us  [swap(): lax.ppermute(x, axis, [(i, i ^ bits) for i in range(lax.axis_size(axis))])]
    ppermute x7, waiting for transfers between devices: 12.7 us -> 11.5 us  [swap(): lax.ppermute(x, axis, [(i, i ^ bits) for i in range(lax.axis_size(axis))])]
    all_to_all x1 -> x2, waiting for transfers between devices: 2.8 us -> 2.91 us  [the longest x1 2.72 us: on_device(): lax.all_to_all(mine64, 'tm', 0, 0, axis_index_groups=across, tiled=True)]
  transfers between devices with their start and end apart: 10 -> 11, of which waited for: 8 -> 8; matrix products, arithmetic and copies ran while one was open for 1% -> 1% of each run, Pallas kernels for 17% -> 24%
where the time goes in v2:
time: 83.3 us; the launch traced here: 82.7 us
  starting transfers between devices  33.2 us (40%)
  Pallas kernels  31.6 us (38%)
  waiting for transfers between devices  14.5 us (17%)
  local copies, waits for them, and re-layouts  2.74 us (3%)
    ppermute x7, starting transfers between devices, swap(): lax.ppermute(x, axis, [(i, i ^ bits) for i in range(lax.axis_size(axis))])  11.6 us
    ppermute x7, waiting for transfers between devices, swap(): lax.ppermute(x, axis, [(i, i ^ bits) for i in range(lax.axis_size(axis))])  11.5 us
    pallas_call x1, Pallas kernels, on_device(): pl.pallas_call(local_kernel, grid=(4,), in_specs=[whole((ROWS, ROWS))] +...  10 us
    pallas_call x1, Pallas kernels, on_device(): pl.pallas_call(rest_kernel, in_specs=[hbm] * 9, out_specs=[pl.BlockSpec(m...  7.29 us
    all_to_all x1, starting transfers between devices, on_device(): x = lax.all_to_all(sent, 'tm', 0, 0, axis_index_groups=lines, tiled=True)  6.69 us
    all_to_all x1, starting transfers between devices, on_device(): lax.all_to_all(mine64, 'tm', 0, 0, axis_index_groups=across, tiled=True)  5.82 us
    all_to_all x1, starting transfers between devices, on_device(): got = lax.all_to_all(back, 'tm', 0, 0, axis_index_groups=lines, tiled=True)  5.72 us
    pallas_call x1, Pallas kernels, on_device(): pl.pallas_call(pack_kernel, in_specs=[hbm] * 5, out_specs=hbm, out_shape=...  5.27 us
  transfers between devices with their start and end apart: 11, of which 8 were waited for; matrix products, arithmetic and copies ran while one was open for 1% of the time, Pallas kernels for 24%

profile of v2, /device:TPU:1, one launch (start us, length us, event | category | flops | bytes accessed | tf_op | source)
XLA Modules:
  0.0 82.7 jit_solution(17477580470197262934)
XLA Ops:
  0.0 5.3 %pack.1 = bf16[8,144,256]{2,1,0:T(8,128)(2,1)} custom-call(bf16[128,512]{1,0:T(8,128)(2,1)} %constant.9.clone.perm_hbm, bf16[512,512]{1,0:T(8,128)(2,1)} %q_ref.1, bf16[512,512]{1,0:T(8,128)(2,1)} %k_hbm.3, bf16[512,512]{1,0:T(8,128)(2,1)} %v_hbm.3, bf16[512,512]{1,0:T(8,128)(2,1)} %g_ref.1), custom_call_target="tpu_custom_call" | custom-call | tf_op jit(solution)/shard_map/pack/pallas_call | solution.py:376
  5.3 6.7 %all-to-all-start = ((bf16[8,144,256]{2,1,0:T(8,128)(2,1)}), bf16[8,144,256]{2,1,0:T(8,128)(2,1)S(1)}, u32[]{:S(2)}, u32[]{:S(2)}) async-start(bf16[8,144,256]{2,1,0:T(8,128)(2,1)} %pack.1), calls=%async_computation | async-start | bytes 1179648 | tf_op jit(solution)/shard_map/all_to_all | solution.py:393
  12.0 10.0 %local.1 = (bf16[2,128,512]{2,1,0:T(8,128)(2,1)}, bf16[384,512]{1,0:T(8,128)(2,1)}, bf16[2,512,512]{2,1,0:T(8,128)(2,1)}, f32[8,128]{1,0:T(8,128)}) custom-call(bf16[512,512]{1,0:T(8,128)(2,1)} %constant.8.clone.perm_ref, bf16[512,512]{1,0:T(8,128)(2,1)} %q_ref.1, bf16[512,512]{1,0:T(8,128)(2,1)} %k_hbm.3, bf16[512,512]{1,0:T(8,128)(2,1)} %v_hbm.3, ...), custom_call_target="tpu_custom_call" | custom-call | flops 12000000000 | bytes 5000000 | tf_op jit(solution)/shard_map/local/pallas_call | solution.py:398
  23.5 5.8 %all-to-all-start.1 = ((bf16[8,64,128]{2,1,0:T(8,128)(2,1)}), bf16[8,64,128]{2,1,0:T(8,128)(2,1)S(1)}, u32[]{:S(2)}, u32[]{:S(2)}) async-start(bf16[8,64,128]{2,1,0:T(8,128)(2,1)} %pick64.1), calls=%async_computation.1 | async-start | bytes 262144 | tf_op jit(solution)/shard_map/all_to_all | solution.py:421
  29.4 1.5 %collective-permute-start = (bf16[256,128]{1,0:T(8,128)(2,1)S(1)}, bf16[256,128]{1,0:T(8,128)(2,1)S(1)}, u32[]{:S(2)}, u32[]{:S(2)}) collective-permute-start(bf16[256,128]{1,0:T(8,128)(2,1)S(1)} %pick16.1.b16_ref), channel_id=1, source_target_pairs={{0,16},{2,18},{4,20},{6,22},{8,24},{10,26},{12,28},{14,30},{16,0},... | collective-permute-start | bytes 196616 | tf_op jit(solution)/shard_map/ppermute | solution.py:360
  30.8 2.0 %collective-permute-done.p16_ref = bf16[256,128]{1,0:T(8,128)(2,1)S(1)} collective-permute-done((bf16[256,128]{1,0:T(8,128)(2,1)S(1)}, bf16[256,128]{1,0:T(8,128)(2,1)S(1)}, u32[]{:S(2)}, u32[]{:S(2)}) %collective-permute-start) | collective-permute-done | bytes 65568 | tf_op jit(solution)/shard_map/ppermute | solution.py:360
  32.8 2.7 %all-to-all-done.1.c64_ref = bf16[8,64,128]{2,1,0:T(8,128)(2,1)S(1)} async-done(((bf16[8,64,128]{2,1,0:T(8,128)(2,1)}), bf16[8,64,128]{2,1,0:T(8,128)(2,1)S(1)}, u32[]{:S(2)}, u32[]{:S(2)}) %all-to-all-start.1) | async-done | bytes 131104 | tf_op jit(solution)/shard_map/all_to_all | solution.py:421
  35.6 3.4 %heads.1 = (f32[8,128,128]{2,1,0:T(8,128)S(1)}, f32[8,128,128]{2,1,0:T(8,128)S(1)}, bf16[256,128]{1,0:T(8,128)(2,1)S(1)}, bf16[8,64,128]{2,1,0:T(8,128)(2,1)}, f32[2,8,128]{2,1,0:T(8,128)S(1)}) custom-call(bf16[8,144,256]{2,1,0:T(8,128)(2,1)S(1)} %all-to-all-done.x_ref, bf16[256,128]{1,0:T(8,128)(2,1)S(1)} %collective-permute-done.p16_ref, ...), custom_call_target="tpu_custom_call" | custom-call | tf_op jit(solution)/shard_map/heads/pallas_call | solution.py:422
  39.0 2.3 %collective-permute-start.2 = (f32[1,2,8,128]{3,2,1,0:T(8,128)S(1)}, f32[1,2,8,128]{3,2,1,0:T(8,128)S(1)}, u32[]{:S(2)}, u32[]{:S(2)}) collective-permute-start(f32[1,2,8,128]{3,2,1,0:T(8,128)S(1)} %bitcast.1), channel_id=1, source_target_pairs={{0,2},{2,0},{4,6},{6,4},{8,10},{10,8},{12,14},{14,12},{16,18},{18,... | collective-permute-start | bytes 24584 | tf_op jit(solution)/shard_map/ppermute | solution.py:360
  41.3 0.8 %collective-permute-done.2 = f32[1,2,8,128]{3,2,1,0:T(8,128)S(1)} collective-permute-done((f32[1,2,8,128]{3,2,1,0:T(8,128)S(1)}, f32[1,2,8,128]{3,2,1,0:T(8,128)S(1)}, u32[]{:S(2)}, u32[]{:S(2)}) %collective-permute-start.2) | collective-permute-done | bytes 8224 | tf_op jit(solution)/shard_map/ppermute | solution.py:360
  42.8 3.4 %all-to-all-start.2 = ((bf16[8,64,128]{2,1,0:T(8,128)(2,1)}), bf16[8,64,128]{2,1,0:T(8,128)(2,1)S(1)}, u32[]{:S(2)}, u32[]{:S(2)}) async-start(bf16[8,64,128]{2,1,0:T(8,128)(2,1)} %get-tuple-element.25), calls=%async_computation.2 | async-start | bytes 262144 | tf_op jit(solution)/shard_map/all_to_all | solution.py:439
  46.2 2.5 %collective-permute-start.4 = (f32[4,2,8,128]{3,2,1,0:T(8,128)S(1)}, f32[4,2,8,128]{3,2,1,0:T(8,128)S(1)}, u32[]{:S(2)}, u32[]{:S(2)}) collective-permute-start(f32[4,2,8,128]{3,2,1,0:T(8,128)S(1)} %pad_maximum_fusion.1), channel_id=1, source_target_pairs={{0,8},{2,10},{4,12},{6,14},{8,0},{10,2},{12,4},{14,6},{16,24},{18,... | collective-permute-start | bytes 98312 | tf_op jit(solution)/shard_map/ppermute | solution.py:360
  48.7 1.3 %collective-permute-start.1 = (bf16[256,128]{1,0:T(8,128)(2,1)S(1)}, bf16[256,128]{1,0:T(8,128)(2,1)S(1)}, u32[]{:S(2)}, u32[]{:S(2)}) collective-permute-start(bf16[256,128]{1,0:T(8,128)(2,1)S(1)} %get-tuple-element.24), channel_id=1, source_target_pairs={{0,16},{2,18},{4,20},{6,22},{8,24},{10,26},{12,28},{14,30},{16,0},... | collective-permute-start | bytes 196616 | tf_op jit(solution)/shard_map/ppermute | solution.py:360
  51.2 1.1 %collective-permute-done.1.got16_ref = bf16[256,128]{1,0:T(8,128)(2,1)S(1)} collective-permute-done((bf16[256,128]{1,0:T(8,128)(2,1)S(1)}, bf16[256,128]{1,0:T(8,128)(2,1)S(1)}, u32[]{:S(2)}, u32[]{:S(2)}) %collective-permute-start.1) | collective-permute-done | bytes 65568 | tf_op jit(solution)/shard_map/ppermute | solution.py:360
  52.3 0.9 %gather.1 = bf16[8,192,128]{2,1,0:T(8,128)(2,1)} custom-call(f32[8,128,128]{2,1,0:T(8,128)S(1)} %get-tuple-element.22.own_ref, f32[8,128,128]{2,1,0:T(8,128)S(1)} %get-tuple-element.23.dq_ref, bf16[256,128]{1,0:T(8,128)(2,1)S(1)} %collective-permute-done.1.got16_ref, bf16[8,64,128]{2,1,0:T(8,128)(2,1)S(1)} %all-to-all-done.2.got64_ref), custom_call_target="tpu_custom_call" | custom-call | tf_op jit(solution)/shard_map/gather/pallas_call | solution.py:440
  53.2 5.7 %all-to-all-start.3 = ((bf16[8,192,128]{2,1,0:T(8,128)(2,1)}), bf16[8,192,128]{2,1,0:T(8,128)(2,1)S(1)}, u32[]{:S(2)}, u32[]{:S(2)}) async-start(bf16[8,192,128]{2,1,0:T(8,128)(2,1)} %gather.1), calls=%async_computation.3 | async-start | bytes 786432 | tf_op jit(solution)/shard_map/all_to_all | solution.py:446
  58.9 7.3 %rest.1 = (bf16[3,128,512]{2,1,0:T(8,128)(2,1)}, bf16[3,192,512]{2,1,0:T(8,128)(2,1)}, bf16[192,1024]{1,0:T(8,128)(2,1)}, bf16[3,20480,512]{2,1,0:T(8,128)(2,1)}) custom-call(f32[8,2,8,128]{3,2,1,0:T(8,128)} %pad_maximum_fusion.st_hbm, bf16[2,128,512]{2,1,0:T(8,128)(2,1)} %get-tuple-element.27.in_hbm, bf16[512,512]{1,0:T(8,128)(2,1)} %k_hbm.3, ...), custom_call_target="tpu_custom_call" | custom-call | flops 5000000000 | bytes 9000000 | tf_op jit(solution)/shard_map/rest/pallas_call | solution.py:450
  66.2 2.5 %collective-permute-start.6 = (bf16[192,1024]{1,0:T(8,128)(2,1)}, bf16[192,1024]{1,0:T(8,128)(2,1)S(1)}, u32[]{:S(2)}, u32[]{:S(2)}) collective-permute-start(bf16[192,1024]{1,0:T(8,128)(2,1)} %get-tuple-element.36), channel_id=1, source_target_pairs={{0,1},{1,0},{2,3},{3,2},{4,5},{5,4},{6,7},{7,6},{8,9},{9,8},{10,11... | collective-permute-start | bytes 1179656 | tf_op jit(solution)/shard_map/ppermute | solution.py:360
  68.8 1.1 %copy-done = bf16[3,192,512]{2,1,0:T(8,128)(2,1)S(1)} copy-done((bf16[3,192,512]{2,1,0:T(8,128)(2,1)S(1)}, bf16[3,192,512]{2,1,0:T(8,128)(2,1)}, u32[]{:S(2)}) %copy-start) | copy-done | bytes 589848
  69.8 1.0 %copy-done.1 = bf16[3,128,512]{2,1,0:T(8,128)(2,1)S(1)} copy-done((bf16[3,128,512]{2,1,0:T(8,128)(2,1)S(1)}, bf16[3,128,512]{2,1,0:T(8,128)(2,1)}, u32[]{:S(2)}) %copy-start.1) | copy-done | bytes 393240
  70.8 2.9 %dil.1 = (f32[64,1024]{1,0:T(8,128)S(1)}, bf16[64,1024]{1,0:T(8,128)(2,1)S(1)}, bf16[192,1024]{1,0:T(8,128)(2,1)S(1)}) custom-call(bf16[128,128]{1,0:T(8,128)(2,1)S(1)} %copy-done.3, bf16[8,192,128]{2,1,0:T(8,128)(2,1)S(1)} %all-to-all-done.3.got_ref, bf16[3,128,512]{2,1,0:T(8,128)(2,1)S(1)} %copy-done.1, bf16[3,192,512]{2,1,0:T(8,128)(2,1)S(1)} %copy-done, ...), custom_call_target="tpu_custom_call" | custom-call | tf_op jit(solution)/shard_map/dil/pallas_call | solution.py:479
  74.5 4.2 %collective-permute-done.6.got_r = bf16[192,1024]{1,0:T(8,128)(2,1)S(1)} collective-permute-done((bf16[192,1024]{1,0:T(8,128)(2,1)}, bf16[192,1024]{1,0:T(8,128)(2,1)S(1)}, u32[]{:S(2)}, u32[]{:S(2)}) %collective-permute-start.6) | collective-permute-done | bytes 393248 | tf_op jit(solution)/shard_map/ppermute | solution.py:360
  78.8 2.8 %collective-permute-done.5.got_d = bf16[64,1024]{1,0:T(8,128)(2,1)S(1)} collective-permute-done((bf16[64,1024]{1,0:T(8,128)(2,1)S(1)}, bf16[64,1024]{1,0:T(8,128)(2,1)S(1)}, u32[]{:S(2)}, u32[]{:S(2)}) %collective-permute-start.5) | collective-permute-done | bytes 131104 | tf_op jit(solution)/shard_map/ppermute | solution.py:360
  81.6 1.1 %last.1 = bf16[256,1024]{1,0:T(8,128)(2,1)} custom-call(bf16[256,256]{1,0:T(8,128)(2,1)S(1)} %copy-done.2, f32[64,1024]{1,0:T(8,128)S(1)} %get-tuple-element.33.keep_d, bf16[64,1024]{1,0:T(8,128)(2,1)S(1)} %collective-permute-done.5.got_d, bf16[192,1024]{1,0:T(8,128)(2,1)S(1)} %get-tuple-element.35.keep_r, bf16[192,1024]{1,0:T(8,128)(2,1)S(1)} %collective-permute-done.6.got_r), custom_call_target="tpu_custom_call" | custom-call | tf_op jit(solution)/shard_map/last/pallas_call | solution.py:492
  (20 shorter events, 4.2 us)
Async XLA Ops:
  0.0 68.8 %copy-start.3 = (bf16[128,128]{1,0:T(8,128)(2,1)S(1)}, bf16[128,128]{1,0:T(8,128)(2,1)}, u32[]{:S(2)}) copy-start(bf16[128,128]{1,0:T(8,128)(2,1)} %constant.10.clone.perm_ref) | copy-start | bytes 98308
  5.3 16.9 %all-to-all-start = ((bf16[8,144,256]{2,1,0:T(8,128)(2,1)}), bf16[8,144,256]{2,1,0:T(8,128)(2,1)S(1)}, u32[]{:S(2)}, u32[]{:S(2)}) async-start(bf16[8,144,256]{2,1,0:T(8,128)(2,1)} %pack.1), calls=%async_computation | async-start | bytes 1179648 | tf_op jit(solution)/shard_map/all_to_all | solution.py:393
  12.0 69.6 %copy-start.2 = (bf16[256,256]{1,0:T(8,128)(2,1)S(1)}, bf16[256,256]{1,0:T(8,128)(2,1)}, u32[]{:S(2)}) copy-start(bf16[256,256]{1,0:T(8,128)(2,1)} %constant.11.clone.perm_ref) | copy-start | bytes 393220
  22.2 0.7 copy-start.4
  23.5 12.0 %all-to-all-start.1 = ((bf16[8,64,128]{2,1,0:T(8,128)(2,1)}), bf16[8,64,128]{2,1,0:T(8,128)(2,1)S(1)}, u32[]{:S(2)}, u32[]{:S(2)}) async-start(bf16[8,64,128]{2,1,0:T(8,128)(2,1)} %pick64.1), calls=%async_computation.1 | async-start | bytes 262144 | tf_op jit(solution)/shard_map/all_to_all | solution.py:421
  29.4 3.5 %collective-permute-start = (bf16[256,128]{1,0:T(8,128)(2,1)S(1)}, bf16[256,128]{1,0:T(8,128)(2,1)S(1)}, u32[]{:S(2)}, u32[]{:S(2)}) collective-permute-start(bf16[256,128]{1,0:T(8,128)(2,1)S(1)} %pick16.1.b16_ref), channel_id=1, source_target_pairs={{0,16},{2,18},{4,20},{6,22},{8,24},{10,26},{12,28},{14,30},{16,0},... | collective-permute-start | bytes 196616 | tf_op jit(solution)/shard_map/ppermute | solution.py:360
  39.0 3.1 %collective-permute-start.2 = (f32[1,2,8,128]{3,2,1,0:T(8,128)S(1)}, f32[1,2,8,128]{3,2,1,0:T(8,128)S(1)}, u32[]{:S(2)}, u32[]{:S(2)}) collective-permute-start(f32[1,2,8,128]{3,2,1,0:T(8,128)S(1)} %bitcast.1), channel_id=1, source_target_pairs={{0,2},{2,0},{4,6},{6,4},{8,10},{10,8},{12,14},{14,12},{16,18},{18,... | collective-permute-start | bytes 24584 | tf_op jit(solution)/shard_map/ppermute | solution.py:360
  42.1 4.1 %collective-permute-start.3 = (f32[2,2,8,128]{3,2,1,0:T(8,128)S(1)}, f32[2,2,8,128]{3,2,1,0:T(8,128)S(1)}, u32[]{:S(2)}, u32[]{:S(2)}) collective-permute-start(f32[2,2,8,128]{3,2,1,0:T(8,128)S(1)} %pad_maximum_fusion.2), channel_id=1, source_target_pairs={{0,4},{2,6},{4,0},{6,2},{8,12},{10,14},{12,8},{14,10},{16,20},{18,... | collective-permute-start | bytes 49160 | tf_op jit(solution)/shard_map/ppermute | solution.py:360
  42.8 9.5 %all-to-all-start.2 = ((bf16[8,64,128]{2,1,0:T(8,128)(2,1)}), bf16[8,64,128]{2,1,0:T(8,128)(2,1)S(1)}, u32[]{:S(2)}, u32[]{:S(2)}) async-start(bf16[8,64,128]{2,1,0:T(8,128)(2,1)} %get-tuple-element.25), calls=%async_computation.2 | async-start | bytes 262144 | tf_op jit(solution)/shard_map/all_to_all | solution.py:439
  46.2 4.4 %collective-permute-start.4 = (f32[4,2,8,128]{3,2,1,0:T(8,128)S(1)}, f32[4,2,8,128]{3,2,1,0:T(8,128)S(1)}, u32[]{:S(2)}, u32[]{:S(2)}) collective-permute-start(f32[4,2,8,128]{3,2,1,0:T(8,128)S(1)} %pad_maximum_fusion.1), channel_id=1, source_target_pairs={{0,8},{2,10},{4,12},{6,14},{8,0},{10,2},{12,4},{14,6},{16,24},{18,... | collective-permute-start | bytes 98312 | tf_op jit(solution)/shard_map/ppermute | solution.py:360
  48.7 3.6 %collective-permute-start.1 = (bf16[256,128]{1,0:T(8,128)(2,1)S(1)}, bf16[256,128]{1,0:T(8,128)(2,1)S(1)}, u32[]{:S(2)}, u32[]{:S(2)}) collective-permute-start(bf16[256,128]{1,0:T(8,128)(2,1)S(1)} %get-tuple-element.24), channel_id=1, source_target_pairs={{0,16},{2,18},{4,20},{6,22},{8,24},{10,26},{12,28},{14,30},{16,0},... | collective-permute-start | bytes 196616 | tf_op jit(solution)/shard_map/ppermute | solution.py:360
  53.2 15.6 %all-to-all-start.3 = ((bf16[8,192,128]{2,1,0:T(8,128)(2,1)}), bf16[8,192,128]{2,1,0:T(8,128)(2,1)S(1)}, u32[]{:S(2)}, u32[]{:S(2)}) async-start(bf16[8,192,128]{2,1,0:T(8,128)(2,1)} %gather.1), calls=%async_computation.3 | async-start | bytes 786432 | tf_op jit(solution)/shard_map/all_to_all | solution.py:446
  66.2 12.5 %collective-permute-start.6 = (bf16[192,1024]{1,0:T(8,128)(2,1)}, bf16[192,1024]{1,0:T(8,128)(2,1)S(1)}, u32[]{:S(2)}, u32[]{:S(2)}) collective-permute-start(bf16[192,1024]{1,0:T(8,128)(2,1)} %get-tuple-element.36), channel_id=1, source_target_pairs={{0,1},{1,0},{2,3},{3,2},{4,5},{5,4},{6,7},{7,6},{8,9},{9,8},{10,11... | collective-permute-start | bytes 1179656 | tf_op jit(solution)/shard_map/ppermute | solution.py:360
  68.8 1.1 %copy-start = (bf16[3,192,512]{2,1,0:T(8,128)(2,1)S(1)}, bf16[3,192,512]{2,1,0:T(8,128)(2,1)}, u32[]{:S(2)}) copy-start(bf16[3,192,512]{2,1,0:T(8,128)(2,1)} %get-tuple-element.31.kept_ref) | copy-start | bytes 1769476
  69.8 1.0 %copy-start.1 = (bf16[3,128,512]{2,1,0:T(8,128)(2,1)S(1)}, bf16[3,128,512]{2,1,0:T(8,128)(2,1)}, u32[]{:S(2)}) copy-start(bf16[3,128,512]{2,1,0:T(8,128)(2,1)} %get-tuple-element.30.dil_ref) | copy-start | bytes 1179652
  73.7 7.8 %collective-permute-start.5 = (bf16[64,1024]{1,0:T(8,128)(2,1)S(1)}, bf16[64,1024]{1,0:T(8,128)(2,1)S(1)}, u32[]{:S(2)}, u32[]{:S(2)}) collective-permute-start(bf16[64,1024]{1,0:T(8,128)(2,1)S(1)} %get-tuple-element.34), channel_id=1, source_target_pairs={{0,1},{1,0},{2,3},{3,2},{4,5},{5,4},{6,7},{7,6},{8,9},{9,8},{10,11... | collective-permute-start | bytes 393224 | tf_op jit(solution)/shard_map/ppermute | solution.py:360

commit v3 on v2

--- a/solution.py
+++ b/solution.py
@@ -16,9 +16,11 @@
 LANES = 128
 HEADS = 8
 STAT_ROWS = 16
+OWN = 1024
+PASSED = DIL + REST // 2
 MIB = 1024 * 1024
 LARGE = 62 * MIB
-TALL = 20 * 1024
+TALL = 15 * 1024
 LOW = -1e30
 
 
@@ -33,23 +35,6 @@
     out = np.zeros((len(index), width), np.float32)
     out[np.arange(len(index)), index] = 1
     return out
-
-
-def order_hot():
-    p = lax.broadcasted_iota(jnp.int32, (ROWS, LANES), 0)
-
-    def skip(i):
-        return i + lax.shift_right_logical(i * 171, 9) + 1
-
-    frame = jnp.where(
-        p < 8,
-        64 * p,
-        jnp.where(p < 32, 16 * skip(p - 8), jnp.where(p < DIL, 4 * skip(p - 32), skip(p - DIL))),
-    )
-    lane = lax.broadcasted_iota(jnp.int32, (ROWS, LANES), 1)
-    return jnp.concatenate(
-        [jnp.where(frame == lane + i * LANES, 1.0, 0.0).astype(BF16) for i in range(ROWS // LANES)], axis=1
-    )
 
 
 def dot_tt(a, b):
@@ -106,6 +91,7 @@
     for s in range(4):
         for i in range(4):
             fetch(s, i).wait()
+    for s in range(4):
         k, v = in_ref[s, 1], in_ref[s, 2]
         block = jnp.concatenate([in_ref[s, 0] * BF16(0.125), k, v, in_ref[s, 3]], axis=1)
         block = dot(perm_ref[...], block).astype(BF16)
@@ -120,19 +106,39 @@
             cols = slice(h * 64, h * 64 + 64)
             x_ref[2 * s + h, :DIL, :] = jnp.concatenate([kd[:, cols], vd[:, cols], qd[:, cols], gd[:, cols]], axis=1)
             x_ref[2 * s + h, DIL:, :] = jnp.concatenate([rows, jnp.zeros_like(rows)], axis=1).astype(BF16)
+    for s in range(4):
         put(s).start()
     for s in range(4):
         put(s).wait()
 
 
-def local_kernel(perm_ref, q_ref, k_ref, v_ref, g_ref, in_ref, dq_ref, sum_ref, token_ref):
-    token_ref[...] = jnp.zeros_like(token_ref)
-    block = jnp.concatenate([q_ref[...] * BF16(0.125), g_ref[...]], axis=1)
+def local_kernel(
+    perm_ref, q_ref, k_ref, v_ref, g_ref, wq_hbm, wk_hbm, wv_hbm,
+    in_ref, kv_ref, dq_ref, sum_ref, w_hbm, w_s, sems,
+):
+    step = pl.program_id(0)
+    loads = [pltpu.make_async_copy(w, w_s.at[i], sems.at[i]) for i, w in enumerate((wq_hbm, wk_hbm, wv_hbm))]
+    store = pltpu.make_async_copy(w_s, w_hbm.at[:, pl.ds(0, OWN)], sems.at[3])
+
+    @pl.when(step == 0)
+    def _():
+        for load in loads:
+            load.start()
+
+    @pl.when(step == 2)
+    def _():
+        for load in loads:
+            load.wait()
+        store.start()
+
+    block = jnp.concatenate([q_ref[...] * BF16(0.125), g_ref[...], k_ref[...], v_ref[...]], axis=1)
     block = dot(perm_ref[...], block).astype(BF16)
     in_ref[0] = block[:DIL, :LANES]
-    in_ref[1] = block[:DIL, LANES:]
-    q, g = block[DIL:, :LANES], block[DIL:, LANES:]
-    k, v = k_ref[...], v_ref[...]
+    in_ref[1] = block[:DIL, LANES : 2 * LANES]
+    q, g = block[DIL:, :LANES], block[DIL:, LANES : 2 * LANES]
+    k, v = block[:, 2 * LANES : 3 * LANES], block[:, 3 * LANES :]
+    kv_ref[0] = k
+    kv_ref[1] = v
     q2, g2 = pair(q), pair(g)
     scores = dot_tt(k, q2)
     grad_prob = dot_tt(v, g2)
@@ -144,13 +150,14 @@
     sum_ref[0] = dot(ds, q2).astype(BF16)
     sum_ref[1] = dot(p.astype(BF16), g2).astype(BF16)
 
-
-def pick16_kernel(x_ref, _, b16_ref):
+    @pl.when(step == 3)
+    def _():
+        store.wait()
+
+
+def pick_kernel(x_ref, _, b16_ref, b64_ref):
     b16_ref[...] = x_ref[:, :32, :LANES].reshape(256, LANES)
-
-
-def pick64_kernel(b16_ref, b64_ref):
-    rows = b16_ref[...].reshape(HEADS, 32, LANES)[:, :16].astype(F32)[:, :8].reshape(64, LANES).astype(BF16)
+    rows = x_ref[:, :16, :LANES].astype(F32)[:, :8, :].reshape(64, LANES).astype(BF16)
     for a in range(HEADS):
         b64_ref[a] = rows
 
@@ -246,24 +253,22 @@
 
 
 def rest_kernel(
-    st_hbm, in_hbm, k_hbm, v_hbm, sum_hbm, dq_hbm, wq_hbm, wk_hbm, wv_hbm,
-    dil_ref, keep_ref, send_ref, w_hbm,
-    st_ref, in_ref, k_ref, v_ref, sum_ref, dq_s, w_s, dk_s, dv_s, sems, out_sems,
+    st_hbm, far_hbm, in_hbm, kv_hbm, sum_hbm, dq_hbm, wq_hbm, wk_hbm, wv_hbm, send_ref, out_hbm,
+    st_ref, in_ref, kv_ref, sum_ref, dq_s, w_s, dk_s, dv_s, pass_s, sems, out_sem,
 ):
-    pairs = [(st_hbm, st_ref), (in_hbm, in_ref), (k_hbm, k_ref), (v_hbm, v_ref), (sum_hbm, sum_ref)]
-    pairs += [(dq_hbm, dq_s)]
+    pairs = [(st_hbm, st_ref.at[pl.ds(0, 4)]), (far_hbm, st_ref.at[pl.ds(4, 4)])]
+    pairs += [(in_hbm, in_ref), (kv_hbm, kv_ref), (sum_hbm, sum_ref), (dq_hbm, dq_s)]
     pairs += [(w, w_s.at[i]) for i, w in enumerate((wq_hbm, wk_hbm, wv_hbm))]
     fetches = [pltpu.make_async_copy(a, b, sems.at[i]) for i, (a, b) in enumerate(pairs)]
     for fetch in fetches:
         fetch.start()
     line = lax.rem(lax.axis_index("tm"), 8)
     head = lax.axis_index("head")
-    perm = order_hot()
     for fetch in fetches[:4]:
         fetch.wait()
     for slab in range(4):
         cols = slice(slab * LANES, (slab + 1) * LANES)
-        k, v = k_ref[:, cols], v_ref[:, cols]
+        k, v = kv_ref[0, :, cols], kv_ref[1, :, cols]
         q2, g2 = pair(in_ref[0, :, cols]), pair(in_ref[1, :, cols])
         scores = dot_tt(k, q2)
         grad_prob = dot_tt(v, g2)
@@ -275,35 +280,35 @@
         p = jnp.exp(scores - jnp.concatenate(lse, axis=1))
         ds = (p * (grad_prob - jnp.concatenate(delta, axis=1))).astype(BF16)
         dq = dot((k * BF16(0.125)).T, ds)
-        dil_ref[0, :, cols] = jnp.concatenate([dq[:64, :DIL], dq[64:, DIL:]], axis=0).T.astype(BF16)
+        pass_s[0, :DIL, cols] = jnp.concatenate([dq[:64, :DIL], dq[64:, DIL:]], axis=0).T.astype(BF16)
         dk, dv = dot(ds, q2), dot(p.astype(BF16), g2)
         if slab == 0:
             fetches[4].wait()
-        dkv = [dk + sum_ref[0, :, cols].astype(F32), dv + sum_ref[1, :, cols].astype(F32)]
-        moved = dot(perm, jnp.concatenate(dkv, axis=1).astype(BF16)).astype(BF16)
-        dil_ref[1, :, cols] = moved[:DIL, :LANES]
-        dil_ref[2, :, cols] = moved[:DIL, LANES:]
-        dk_s[:, cols] = moved[DIL:, :LANES]
-        dv_s[:, cols] = moved[DIL:, LANES:]
-    for fetch in fetches[5:]:
-        fetch.wait()
-    puts = [pltpu.make_async_copy(w_s.at[i], w_hbm.at[i, pl.ds(0, 1024)], out_sems.at[i]) for i in range(3)]
-    for put in puts:
-        put.start()
+        dk = (dk + sum_ref[0, :, cols].astype(F32)).astype(BF16)
+        dv = (dv + sum_ref[1, :, cols].astype(F32)).astype(BF16)
+        pass_s[1, :DIL, cols] = dk[:DIL]
+        pass_s[2, :DIL, cols] = dv[:DIL]
+        dk_s[:, cols] = dk[DIL:]
+        dv_s[:, cols] = dv[DIL:]
     half = REST // 2
     keep = pl.ds(pl.multiple_of(head * half, half), half)
     send = pl.ds(pl.multiple_of((1 - head) * half, half), half)
+    fetches[5].wait()
     for i, grad in enumerate((dq_s, dk_s, dv_s)):
-        keep_ref[i] = grad[keep, :]
+        pass_s[i, DIL:, :] = grad[keep, :]
+    put = pltpu.make_async_copy(pass_s, out_hbm.at[:, pl.ds(0, PASSED)], out_sem)
+    put.start()
+    for fetch in fetches[6:]:
+        fetch.wait()
     out = dot_tt(dq_s[send, :], w_s[0]) + dot_tt(dk_s[send, :], w_s[1]) + dot_tt(dv_s[send, :], w_s[2])
     send_ref[...] = out.astype(BF16)
-    for put in puts:
-        put.wait()
-
-
-def dil_kernel(perm_ref, got_ref, dil_ref, kept_ref, w_hbm, keep_ref, send_ref, keep_r, out_s, w_s, sems):
+    put.wait()
+
+
+def dil_kernel(perm_ref, got_ref, pass_hbm, w_hbm, keep_ref, send_ref, keep_r, out_s, pass_s, w_s, sems):
     head = lax.axis_index("head")
-    fetches = [pltpu.make_async_copy(w_hbm.at[i, pl.ds(0, 1024)], w_s.at[i], sems.at[i]) for i in range(3)]
+    fetches = [pltpu.make_async_copy(pass_hbm.at[:, pl.ds(0, PASSED)], pass_s, sems.at[3])]
+    fetches += [pltpu.make_async_copy(w_hbm.at[i, pl.ds(0, OWN)], w_s.at[i], sems.at[i]) for i in range(3)]
     for fetch in fetches:
         fetch.start()
 
@@ -316,11 +321,12 @@
         [both([got_ref[h, DIL:, s * 64 : s * 64 + 64].astype(F32) for h in range(HEADS)]) for s in range(2)], axis=0
     )
     perm = perm_ref[...]
-    grads = [dot(perm, (grad + dil_ref[i].astype(F32)).astype(BF16)).astype(BF16) for i, grad in enumerate((dq, dk, dv))]
+    fetches[0].wait()
+    grads = [dot(perm, (grad + pass_s[i, :DIL, :].astype(F32)).astype(BF16)).astype(BF16) for i, grad in enumerate((dq, dk, dv))]
     out = None
     for i, rows in enumerate(grads):
-        fetches[i].wait()
-        part = dot_tt(jnp.concatenate([rows, kept_ref[i]], axis=0), w_s[i])
+        fetches[1 + i].wait()
+        part = dot_tt(jnp.concatenate([rows, pass_s[i, DIL:, :]], axis=0), w_s[i])
         out = part if out is None else out + part
     out_s[...] = out[:DIL]
     keep_r[...] = out[DIL:].astype(BF16)
@@ -365,6 +371,7 @@
     lines = [[a * 8 + j for j in range(8)] for a in range(size // 8)]
     across = [[b * 64 + a * 8 + j for a in range(8)] for b in range(size // 64) for j in range(8)]
     hbm = pl.BlockSpec(memory_space=pltpu.HBM)
+    vmem = pl.BlockSpec(memory_space=pltpu.VMEM)
     dil, order = frame_order()
     perm = jnp.asarray(one_hot(order, ROWS), BF16)
     perm_first = jnp.asarray(one_hot(order[:DIL], ROWS), BF16)
@@ -395,29 +402,38 @@
     def stack_spec(planes, rows):
         return pl.BlockSpec((planes, rows, LANES), lambda s: (0, 0, s))
 
-    ins, dq1, sums, token = pl.pallas_call(
+    ins, kv, dq1, sums, weights = pl.pallas_call(
         local_kernel,
         grid=(4,),
-        in_specs=[whole((ROWS, ROWS))] + [slab_spec(ROWS)] * 4,
-        out_specs=[stack_spec(2, DIL), slab_spec(REST), stack_spec(2, ROWS), whole((8, LANES))],
+        in_specs=[whole((ROWS, ROWS))] + [slab_spec(ROWS)] * 4 + [hbm] * 3,
+        out_specs=[
+            stack_spec(2, DIL),
+            stack_spec(2, ROWS),
+            slab_spec(REST),
+            stack_spec(2, ROWS),
+            hbm,
+        ],
+        scratch_shapes=[pltpu.VMEM((3, OWN, 512), BF16), pltpu.SemaphoreType.DMA((4,))],
         out_shape=[
             shape((2, DIL, 512), BF16),
+            shape((2, ROWS, 512), BF16),
             shape((REST, 512), BF16),
             shape((2, ROWS, 512), BF16),
-            shape((8, LANES), F32),
+            shape((3, TALL, 512), BF16),
         ],
         compiler_params=params(),
         cost_estimate=cost(12_000_000_000, 5_000_000, 1_600_000),
         name="local",
-    )(perm, queries, keys, values, grad_attn)
-
-    mine16 = pl.pallas_call(
-        pick16_kernel, out_shape=shape((256, LANES), BF16), compiler_params=params(8 * MIB), name="pick16"
-    )(x, token)
+    )(perm, queries, keys, values, grad_attn, w_query, w_key, w_value)
+
+    mine16, mine64 = pl.pallas_call(
+        pick_kernel,
+        in_specs=[vmem, hbm],
+        out_shape=[shape((256, LANES), BF16), shape((8, 64, LANES), BF16)],
+        compiler_params=params(32 * MIB),
+        name="pick",
+    )(x, weights)
     p16 = swap(mine16, "tm", 8)
-    mine64 = pl.pallas_call(
-        pick64_kernel, out_shape=shape((8, 64, LANES), BF16), compiler_params=params(8 * MIB), name="pick64"
-    )(mine16)
     c64 = lax.all_to_all(mine64, "tm", 0, 0, axis_index_groups=across, tiled=True)
     own, dq_own, part16, part64, stat = pl.pallas_call(
         head_kernel,
@@ -433,8 +449,9 @@
     )(x, p16, c64)
 
     st = stat[None]
-    for bit in (1, 2, 4):
+    for bit in (1, 2):
         st = jnp.concatenate([st, swap(st, "tm", bit)], axis=0)
+    st_far = swap(st, "tm", 4)
     got16 = swap(part16, "tm", 8)
     got64 = lax.all_to_all(part64, "tm", 0, 0, axis_index_groups=across, tiled=True)
     back = pl.pallas_call(
@@ -445,49 +462,44 @@
     )(own, dq_own, got16, got64)
     got = lax.all_to_all(back, "tm", 0, 0, axis_index_groups=lines, tiled=True)
 
-    vmem = pl.BlockSpec(memory_space=pltpu.VMEM)
     half = REST // 2
-    dil_own, kept, send_r, weights = pl.pallas_call(
+    send_r, passed = pl.pallas_call(
         rest_kernel,
         in_specs=[hbm] * 9,
-        out_specs=[pl.BlockSpec(memory_space=pltpu.VMEM)] * 3 + [hbm],
-        out_shape=[
-            shape((3, DIL, 512), BF16),
-            shape((3, half, 512), BF16),
-            shape((half, 1024), BF16),
-            shape((3, TALL, 512), BF16),
-        ],
+        out_specs=[vmem, hbm],
+        out_shape=[shape((half, 1024), BF16), shape((3, TALL, 512), BF16)],
         scratch_shapes=[
             pltpu.VMEM((8, 2, HEADS, DIL), F32),
             pltpu.VMEM((2, DIL, 512), BF16),
-            pltpu.VMEM((ROWS, 512), BF16),
-            pltpu.VMEM((ROWS, 512), BF16),
+            pltpu.VMEM((2, ROWS, 512), BF16),
             pltpu.VMEM((2, ROWS, 512), BF16),
             pltpu.VMEM((REST, 512), BF16),
-            pltpu.VMEM((3, 1024, 512), BF16),
+            pltpu.VMEM((3, OWN, 512), BF16),
             pltpu.VMEM((REST, 512), BF16),
             pltpu.VMEM((REST, 512), BF16),
+            pltpu.VMEM((3, PASSED, 512), BF16),
             pltpu.SemaphoreType.DMA((9,)),
-            pltpu.SemaphoreType.DMA((3,)),
+            pltpu.SemaphoreType.DMA,
         ],
         compiler_params=params(),
         cost_estimate=cost(5_000_000_000, 9_000_000, 600_000),
         name="rest",
-    )(st, ins, keys, values, sums, dq1, w_query, w_key, w_value)
+    )(st, st_far, ins, kv, sums, dq1, w_query, w_key, w_value)
     got_r = swap(send_r, "head", 1)
 
     keep_d, send_d, keep_r = pl.pallas_call(
         dil_kernel,
-        in_specs=[vmem] * 4 + [hbm],
+        in_specs=[vmem] * 2 + [hbm] * 2,
         out_shape=[shape((DIL // 2, 1024), F32), shape((DIL // 2, 1024), BF16), shape((half, 1024), BF16)],
         scratch_shapes=[
             pltpu.VMEM((DIL, 1024), F32),
-            pltpu.VMEM((3, 1024, 512), BF16),
-            pltpu.SemaphoreType.DMA((3,)),
+            pltpu.VMEM((3, PASSED, 512), BF16),
+            pltpu.VMEM((3, OWN, 512), BF16),
+            pltpu.SemaphoreType.DMA((4,)),
         ],
-        compiler_params=params(12 * MIB),
+        compiler_params=params(24 * MIB),
         name="dil",
-    )(perm_dil, got, dil_own, kept, weights)
+    )(perm_dil, got, passed, weights)
     got_d = swap(send_d, "head", 1)
     return pl.pallas_call(
         last_kernel,

time: 83.3 us -> 79.3 us (0.952)
  local copies, waits for them, and re-layouts: 2.74 us -> 0.61 us
  Pallas kernels: 31.6 us -> 29.8 us
    unnamed x10 -> x8, local copies, waits for them, and re-layouts: 2.74 us -> 0.61 us
    pallas_call x4 -> x3, Pallas kernels: 10.9 us -> 9.5 us  [the longest x1 5.56 us: on_device(): pl.pallas_call(rest_kernel, in_specs=[hbm] * 9, out_specs=[vmem, hbm], ou...]
    ppermute x7, waiting for transfers between devices: 11.5 us -> 10.3 us  [swap(): lax.ppermute(x, axis, [(i, i ^ bits) for i in range(lax.axis_size(axis))])]
    ppermute x7, starting transfers between devices: 11.6 us -> 12.8 us  [swap(): lax.ppermute(x, axis, [(i, i ^ bits) for i in range(lax.axis_size(axis))])]
    all_to_all x1, waiting for transfers between devices: 0.04 us -> 1.17 us  [on_device(): lax.all_to_all(part64, 'tm', 0, 0, axis_index_groups=across, tiled=True)]
  transfers between devices with their start and end apart: 11 -> 11, of which waited for: 8 -> 7; matrix products, arithmetic and copies ran while one was open for 1% -> 0% of each run, Pallas kernels for 24% -> 25%
where the time goes in v3:
time: 79.3 us; the launch traced here: 78.8 us
  starting transfers between devices  34 us (43%)
  Pallas kernels  29.8 us (38%)
  waiting for transfers between devices  14.3 us (18%)
    ppermute x7, starting transfers between devices, swap(): lax.ppermute(x, axis, [(i, i ^ bits) for i in range(lax.axis_size(axis))])  12.8 us
    ppermute x7, waiting for transfers between devices, swap(): lax.ppermute(x, axis, [(i, i ^ bits) for i in range(lax.axis_size(axis))])  10.3 us
    pallas_call x1, Pallas kernels, on_device(): pl.pallas_call(local_kernel, grid=(4,), in_specs=[whole((ROWS, ROWS))] +...  10.2 us
    all_to_all x1, starting transfers between devices, on_device(): x = lax.all_to_all(sent, 'tm', 0, 0, axis_index_groups=lines, tiled=True)  6.69 us
    all_to_all x1, starting transfers between devices, on_device(): lax.all_to_all(mine64, 'tm', 0, 0, axis_index_groups=across, tiled=True)  5.84 us
    pallas_call x1, Pallas kernels, on_device(): pl.pallas_call(rest_kernel, in_specs=[hbm] * 9, out_specs=[vmem, hbm], ou...  5.56 us
    all_to_all x1, starting transfers between devices, on_device(): got = lax.all_to_all(back, 'tm', 0, 0, axis_index_groups=lines, tiled=True)  5.24 us
    pallas_call x1, Pallas kernels, on_device(): pl.pallas_call(pack_kernel, in_specs=[hbm] * 5, out_specs=hbm, out_shape=...  4.68 us
  transfers between devices with their start and end apart: 11, of which 7 were waited for; matrix products, arithmetic and copies ran while one was open for 0% of the time, Pallas kernels for 25%

profile of v3, /device:TPU:1, one launch (start us, length us, event | category | flops | bytes accessed | tf_op | source)
XLA Modules:
  0.0 78.8 jit_solution(9846314616521752092)
XLA Ops:
  0.0 4.7 %pack.1 = bf16[8,144,256]{2,1,0:T(8,128)(2,1)} custom-call(bf16[128,512]{1,0:T(8,128)(2,1)} %constant.9.clone.perm_hbm, bf16[512,512]{1,0:T(8,128)(2,1)} %q_ref.1, bf16[512,512]{1,0:T(8,128)(2,1)} %k_ref.1, bf16[512,512]{1,0:T(8,128)(2,1)} %v_ref.1, bf16[512,512]{1,0:T(8,128)(2,1)} %g_ref.1), custom_call_target="tpu_custom_call" | custom-call | tf_op jit(solution)/shard_map/pack/pallas_call | solution.py:383
  4.7 6.7 %all-to-all-start = ((bf16[8,144,256]{2,1,0:T(8,128)(2,1)}), bf16[8,144,256]{2,1,0:T(8,128)(2,1)S(1)}, u32[]{:S(2)}, u32[]{:S(2)}) async-start(bf16[8,144,256]{2,1,0:T(8,128)(2,1)} %pack.1), calls=%async_computation | async-start | bytes 1179648 | tf_op jit(solution)/shard_map/all_to_all | solution.py:400
  11.4 10.2 %local.1 = (bf16[2,128,512]{2,1,0:T(8,128)(2,1)}, bf16[2,512,512]{2,1,0:T(8,128)(2,1)}, bf16[384,512]{1,0:T(8,128)(2,1)}, bf16[2,512,512]{2,1,0:T(8,128)(2,1)}, bf16[3,15360,512]{2,1,0:T(8,128)(2,1)}) custom-call(bf16[512,512]{1,0:T(8,128)(2,1)} %constant.8.clone.perm_ref, bf16[512,512]{1,0:T(8,128)(2,1)} %q_ref.1, bf16[512,512]{1,0:T(8,128)(2,1)} %k_ref.1, ...), custom_call_target="tpu_custom_call" | custom-call | flops 12000000000 | bytes 5000000 | tf_op jit(solution)/shard_map/local/pallas_call | solution.py:405
  21.6 0.7 pick.1
  22.3 5.8 %all-to-all-start.1 = ((bf16[8,64,128]{2,1,0:T(8,128)(2,1)}), bf16[8,64,128]{2,1,0:T(8,128)(2,1)S(1)}, u32[]{:S(2)}, u32[]{:S(2)}) async-start(bf16[8,64,128]{2,1,0:T(8,128)(2,1)} %get-tuple-element.24), calls=%async_computation.1 | async-start | bytes 262144 | tf_op jit(solution)/shard_map/all_to_all | solution.py:437
  28.1 1.5 %collective-permute-start = (bf16[256,128]{1,0:T(8,128)(2,1)S(1)}, bf16[256,128]{1,0:T(8,128)(2,1)S(1)}, u32[]{:S(2)}, u32[]{:S(2)}) collective-permute-start(bf16[256,128]{1,0:T(8,128)(2,1)S(1)} %get-tuple-element.23), channel_id=1, source_target_pairs={{0,16},{2,18},{4,20},{6,22},{8,24},{10,26},{12,28},{14,30},{16,0},... | collective-permute-start | bytes 196616 | tf_op jit(solution)/shard_map/ppermute | solution.py:366
  29.6 2.0 %collective-permute-done.p16_ref = bf16[256,128]{1,0:T(8,128)(2,1)S(1)} collective-permute-done((bf16[256,128]{1,0:T(8,128)(2,1)S(1)}, bf16[256,128]{1,0:T(8,128)(2,1)S(1)}, u32[]{:S(2)}, u32[]{:S(2)}) %collective-permute-start) | collective-permute-done | bytes 65568 | tf_op jit(solution)/shard_map/ppermute | solution.py:366
  31.6 2.8 %all-to-all-done.1.c64_ref = bf16[8,64,128]{2,1,0:T(8,128)(2,1)S(1)} async-done(((bf16[8,64,128]{2,1,0:T(8,128)(2,1)}), bf16[8,64,128]{2,1,0:T(8,128)(2,1)S(1)}, u32[]{:S(2)}, u32[]{:S(2)}) %all-to-all-start.1) | async-done | bytes 131104 | tf_op jit(solution)/shard_map/all_to_all | solution.py:437
  34.4 3.4 %heads.1 = (f32[8,128,128]{2,1,0:T(8,128)S(1)}, f32[8,128,128]{2,1,0:T(8,128)S(1)}, bf16[256,128]{1,0:T(8,128)(2,1)S(1)}, bf16[8,64,128]{2,1,0:T(8,128)(2,1)}, f32[2,8,128]{2,1,0:T(8,128)S(1)}) custom-call(bf16[8,144,256]{2,1,0:T(8,128)(2,1)S(1)} %all-to-all-done.x_ref, bf16[256,128]{1,0:T(8,128)(2,1)S(1)} %collective-permute-done.p16_ref, ...), custom_call_target="tpu_custom_call" | custom-call | tf_op jit(solution)/shard_map/heads/pallas_call | solution.py:438
  37.9 2.2 %collective-permute-start.2 = (f32[1,2,8,128]{3,2,1,0:T(8,128)S(1)}, f32[1,2,8,128]{3,2,1,0:T(8,128)S(1)}, u32[]{:S(2)}, u32[]{:S(2)}) collective-permute-start(f32[1,2,8,128]{3,2,1,0:T(8,128)S(1)} %bitcast.1), channel_id=1, source_target_pairs={{0,2},{2,0},{4,6},{6,4},{8,10},{10,8},{12,14},{14,12},{16,18},{18,... | collective-permute-start | bytes 24584 | tf_op jit(solution)/shard_map/ppermute | solution.py:366
  40.0 3.4 %all-to-all-start.2 = ((bf16[8,64,128]{2,1,0:T(8,128)(2,1)}), bf16[8,64,128]{2,1,0:T(8,128)(2,1)S(1)}, u32[]{:S(2)}, u32[]{:S(2)}) async-start(bf16[8,64,128]{2,1,0:T(8,128)(2,1)} %get-tuple-element.28), calls=%async_computation.2 | async-start | bytes 262144 | tf_op jit(solution)/shard_map/all_to_all | solution.py:456
  43.4 1.0 %collective-permute-start.3 = (f32[2,2,8,128]{3,2,1,0:T(8,128)S(1)}, f32[2,2,8,128]{3,2,1,0:T(8,128)S(1)}, u32[]{:S(2)}, u32[]{:S(2)}) collective-permute-start(f32[2,2,8,128]{3,2,1,0:T(8,128)S(1)} %pad_maximum_fusion.1), channel_id=1, source_target_pairs={{0,4},{2,6},{4,0},{6,2},{8,12},{10,14},{12,8},{14,10},{16,20},{18,... | collective-permute-start | bytes 49160 | tf_op jit(solution)/shard_map/ppermute | solution.py:366
  44.4 1.3 %collective-permute-start.1 = (bf16[256,128]{1,0:T(8,128)(2,1)S(1)}, bf16[256,128]{1,0:T(8,128)(2,1)S(1)}, u32[]{:S(2)}, u32[]{:S(2)}) collective-permute-start(bf16[256,128]{1,0:T(8,128)(2,1)S(1)} %get-tuple-element.27), channel_id=1, source_target_pairs={{0,16},{2,18},{4,20},{6,22},{8,24},{10,26},{12,28},{14,30},{16,0},... | collective-permute-start | bytes 196616 | tf_op jit(solution)/shard_map/ppermute | solution.py:366
  46.1 2.4 %collective-permute-start.4 = (f32[4,2,8,128]{3,2,1,0:T(8,128)S(1)}, f32[4,2,8,128]{3,2,1,0:T(8,128)S(1)}, u32[]{:S(2)}, u32[]{:S(2)}) collective-permute-start(f32[4,2,8,128]{3,2,1,0:T(8,128)S(1)} %pad_maximum_fusion.st_hbm), channel_id=1, source_target_pairs={{0,8},{2,10},{4,12},{6,14},{8,0},{10,2},{12,4},{14,6},{16,24},{18,... | collective-permute-start | bytes 98312 | tf_op jit(solution)/shard_map/ppermute | solution.py:366
  48.8 1.2 %all-to-all-done.2.got64_ref = bf16[8,64,128]{2,1,0:T(8,128)(2,1)S(1)} async-done(((bf16[8,64,128]{2,1,0:T(8,128)(2,1)}), bf16[8,64,128]{2,1,0:T(8,128)(2,1)S(1)}, u32[]{:S(2)}, u32[]{:S(2)}) %all-to-all-start.2) | async-done | bytes 131104 | tf_op jit(solution)/shard_map/all_to_all | solution.py:456
  50.0 0.9 %gather.1 = bf16[8,192,128]{2,1,0:T(8,128)(2,1)} custom-call(f32[8,128,128]{2,1,0:T(8,128)S(1)} %get-tuple-element.25.own_ref, f32[8,128,128]{2,1,0:T(8,128)S(1)} %get-tuple-element.26.dq_ref, bf16[256,128]{1,0:T(8,128)(2,1)S(1)} %collective-permute-done.1.got16_ref, bf16[8,64,128]{2,1,0:T(8,128)(2,1)S(1)} %all-to-all-done.2.got64_ref), custom_call_target="tpu_custom_call" | custom-call | tf_op jit(solution)/shard_map/gather/pallas_call | solution.py:457
  50.9 5.2 %all-to-all-start.3 = ((bf16[8,192,128]{2,1,0:T(8,128)(2,1)}), bf16[8,192,128]{2,1,0:T(8,128)(2,1)S(1)}, u32[]{:S(2)}, u32[]{:S(2)}) async-start(bf16[8,192,128]{2,1,0:T(8,128)(2,1)} %gather.1), calls=%async_computation.3 | async-start | bytes 786432 | tf_op jit(solution)/shard_map/all_to_all | solution.py:463
  56.8 5.6 %rest.1 = (bf16[192,1024]{1,0:T(8,128)(2,1)}, bf16[3,15360,512]{2,1,0:T(8,128)(2,1)}) custom-call(f32[4,2,8,128]{3,2,1,0:T(8,128)} %copy-done.2, f32[4,2,8,128]{3,2,1,0:T(8,128)} %copy-done.3, bf16[2,128,512]{2,1,0:T(8,128)(2,1)} %get-tuple-element.30.in_hbm, bf16[2,512,512]{2,1,0:T(8,128)(2,1)} %get-tuple-element.31.kv_hbm, ...), custom_call_target="tpu_custom_call" | custom-call | flops 5000000000 | bytes 9000000 | tf_op jit(solution)/shard_map/rest/pallas_call | solution.py:466
  62.3 2.5 %collective-permute-start.6 = (bf16[192,1024]{1,0:T(8,128)(2,1)}, bf16[192,1024]{1,0:T(8,128)(2,1)S(1)}, u32[]{:S(2)}, u32[]{:S(2)}) collective-permute-start(bf16[192,1024]{1,0:T(8,128)(2,1)} %get-tuple-element.38), channel_id=1, source_target_pairs={{0,1},{1,0},{2,3},{3,2},{4,5},{5,4},{6,7},{7,6},{8,9},{9,8},{10,11... | collective-permute-start | bytes 1179656 | tf_op jit(solution)/shard_map/ppermute | solution.py:366
  64.9 3.3 %dil.1 = (f32[64,1024]{1,0:T(8,128)S(1)}, bf16[64,1024]{1,0:T(8,128)(2,1)S(1)}, bf16[192,1024]{1,0:T(8,128)(2,1)S(1)}) custom-call(bf16[128,128]{1,0:T(8,128)(2,1)S(1)} %copy-done.1, bf16[8,192,128]{2,1,0:T(8,128)(2,1)S(1)} %all-to-all-done.3.got_ref, bf16[3,15360,512]{2,1,0:T(8,128)(2,1)} %get-tuple-element.34.pass_hbm, ...), custom_call_target="tpu_custom_call" | custom-call | tf_op jit(solution)/shard_map/dil/pallas_call | solution.py:490
  68.1 1.9 %collective-permute-start.5 = (bf16[64,1024]{1,0:T(8,128)(2,1)S(1)}, bf16[64,1024]{1,0:T(8,128)(2,1)S(1)}, u32[]{:S(2)}, u32[]{:S(2)}) collective-permute-start(bf16[64,1024]{1,0:T(8,128)(2,1)S(1)} %get-tuple-element.36), channel_id=1, source_target_pairs={{0,1},{1,0},{2,3},{3,2},{4,5},{5,4},{6,7},{7,6},{8,9},{9,8},{10,11... | collective-permute-start | bytes 393224 | tf_op jit(solution)/shard_map/ppermute | solution.py:366
  70.0 4.8 %collective-permute-done.6.got_r = bf16[192,1024]{1,0:T(8,128)(2,1)S(1)} collective-permute-done((bf16[192,1024]{1,0:T(8,128)(2,1)}, bf16[192,1024]{1,0:T(8,128)(2,1)S(1)}, u32[]{:S(2)}, u32[]{:S(2)}) %collective-permute-start.6) | collective-permute-done | bytes 393248 | tf_op jit(solution)/shard_map/ppermute | solution.py:366
  74.9 2.8 %collective-permute-done.5.got_d = bf16[64,1024]{1,0:T(8,128)(2,1)S(1)} collective-permute-done((bf16[64,1024]{1,0:T(8,128)(2,1)S(1)}, bf16[64,1024]{1,0:T(8,128)(2,1)S(1)}, u32[]{:S(2)}, u32[]{:S(2)}) %collective-permute-start.5) | collective-permute-done | bytes 131104 | tf_op jit(solution)/shard_map/ppermute | solution.py:366
  77.7 1.1 %last.1 = bf16[256,1024]{1,0:T(8,128)(2,1)} custom-call(bf16[256,256]{1,0:T(8,128)(2,1)S(1)} %copy-done, f32[64,1024]{1,0:T(8,128)S(1)} %get-tuple-element.35.keep_d, bf16[64,1024]{1,0:T(8,128)(2,1)S(1)} %collective-permute-done.5.got_d, bf16[192,1024]{1,0:T(8,128)(2,1)S(1)} %get-tuple-element.37.keep_r, bf16[192,1024]{1,0:T(8,128)(2,1)S(1)} %collective-permute-done.6.got_r), custom_call_target="tpu_custom_call" | custom-call | tf_op jit(solution)/shard_map/last/pallas_call | solution.py:504
  (16 shorter events, 1.2 us)
Async XLA Ops:
  4.7 16.9 %all-to-all-start = ((bf16[8,144,256]{2,1,0:T(8,128)(2,1)}), bf16[8,144,256]{2,1,0:T(8,128)(2,1)S(1)}, u32[]{:S(2)}, u32[]{:S(2)}) async-start(bf16[8,144,256]{2,1,0:T(8,128)(2,1)} %pack.1), calls=%async_computation | async-start | bytes 1179648 | tf_op jit(solution)/shard_map/all_to_all | solution.py:400
  11.4 53.5 %copy-start.1 = (bf16[128,128]{1,0:T(8,128)(2,1)S(1)}, bf16[128,128]{1,0:T(8,128)(2,1)}, u32[]{:S(2)}) copy-start(bf16[128,128]{1,0:T(8,128)(2,1)} %constant.10.clone.perm_ref) | copy-start | bytes 98308
  22.3 12.1 %all-to-all-start.1 = ((bf16[8,64,128]{2,1,0:T(8,128)(2,1)}), bf16[8,64,128]{2,1,0:T(8,128)(2,1)S(1)}, u32[]{:S(2)}, u32[]{:S(2)}) async-start(bf16[8,64,128]{2,1,0:T(8,128)(2,1)} %get-tuple-element.24), calls=%async_computation.1 | async-start | bytes 262144 | tf_op jit(solution)/shard_map/all_to_all | solution.py:437
  28.1 3.5 %collective-permute-start = (bf16[256,128]{1,0:T(8,128)(2,1)S(1)}, bf16[256,128]{1,0:T(8,128)(2,1)S(1)}, u32[]{:S(2)}, u32[]{:S(2)}) collective-permute-start(bf16[256,128]{1,0:T(8,128)(2,1)S(1)} %get-tuple-element.23), channel_id=1, source_target_pairs={{0,16},{2,18},{4,20},{6,22},{8,24},{10,26},{12,28},{14,30},{16,0},... | collective-permute-start | bytes 196616 | tf_op jit(solution)/shard_map/ppermute | solution.py:366
  37.9 5.5 %collective-permute-start.2 = (f32[1,2,8,128]{3,2,1,0:T(8,128)S(1)}, f32[1,2,8,128]{3,2,1,0:T(8,128)S(1)}, u32[]{:S(2)}, u32[]{:S(2)}) collective-permute-start(f32[1,2,8,128]{3,2,1,0:T(8,128)S(1)} %bitcast.1), channel_id=1, source_target_pairs={{0,2},{2,0},{4,6},{6,4},{8,10},{10,8},{12,14},{14,12},{16,18},{18,... | collective-permute-start | bytes 24584 | tf_op jit(solution)/shard_map/ppermute | solution.py:366
  40.0 10.0 %all-to-all-start.2 = ((bf16[8,64,128]{2,1,0:T(8,128)(2,1)}), bf16[8,64,128]{2,1,0:T(8,128)(2,1)S(1)}, u32[]{:S(2)}, u32[]{:S(2)}) async-start(bf16[8,64,128]{2,1,0:T(8,128)(2,1)} %get-tuple-element.28), calls=%async_computation.2 | async-start | bytes 262144 | tf_op jit(solution)/shard_map/all_to_all | solution.py:456
  43.4 2.7 %collective-permute-start.3 = (f32[2,2,8,128]{3,2,1,0:T(8,128)S(1)}, f32[2,2,8,128]{3,2,1,0:T(8,128)S(1)}, u32[]{:S(2)}, u32[]{:S(2)}) collective-permute-start(f32[2,2,8,128]{3,2,1,0:T(8,128)S(1)} %pad_maximum_fusion.1), channel_id=1, source_target_pairs={{0,4},{2,6},{4,0},{6,2},{8,12},{10,14},{12,8},{14,10},{16,20},{18,... | collective-permute-start | bytes 49160 | tf_op jit(solution)/shard_map/ppermute | solution.py:366
  44.4 4.4 %collective-permute-start.1 = (bf16[256,128]{1,0:T(8,128)(2,1)S(1)}, bf16[256,128]{1,0:T(8,128)(2,1)S(1)}, u32[]{:S(2)}, u32[]{:S(2)}) collective-permute-start(bf16[256,128]{1,0:T(8,128)(2,1)S(1)} %get-tuple-element.27), channel_id=1, source_target_pairs={{0,16},{2,18},{4,20},{6,22},{8,24},{10,26},{12,28},{14,30},{16,0},... | collective-permute-start | bytes 196616 | tf_op jit(solution)/shard_map/ppermute | solution.py:366
  46.1 10.1 %copy-start.2 = (f32[4,2,8,128]{3,2,1,0:T(8,128)}, f32[4,2,8,128]{3,2,1,0:T(8,128)S(1)}, u32[]{:S(2)}) copy-start(f32[4,2,8,128]{3,2,1,0:T(8,128)S(1)} %pad_maximum_fusion.st_hbm) | copy-start | bytes 98308
  46.1 10.0 %collective-permute-start.4 = (f32[4,2,8,128]{3,2,1,0:T(8,128)S(1)}, f32[4,2,8,128]{3,2,1,0:T(8,128)S(1)}, u32[]{:S(2)}, u32[]{:S(2)}) collective-permute-start(f32[4,2,8,128]{3,2,1,0:T(8,128)S(1)} %pad_maximum_fusion.st_hbm), channel_id=1, source_target_pairs={{0,8},{2,10},{4,12},{6,14},{8,0},{10,2},{12,4},{14,6},{16,24},{18,... | collective-permute-start | bytes 98312 | tf_op jit(solution)/shard_map/ppermute | solution.py:366
  50.9 14.0 %all-to-all-start.3 = ((bf16[8,192,128]{2,1,0:T(8,128)(2,1)}), bf16[8,192,128]{2,1,0:T(8,128)(2,1)S(1)}, u32[]{:S(2)}, u32[]{:S(2)}) async-start(bf16[8,192,128]{2,1,0:T(8,128)(2,1)} %gather.1), calls=%async_computation.3 | async-start | bytes 786432 | tf_op jit(solution)/shard_map/all_to_all | solution.py:463
  56.1 0.6 copy-start.3
  62.3 12.5 %collective-permute-start.6 = (bf16[192,1024]{1,0:T(8,128)(2,1)}, bf16[192,1024]{1,0:T(8,128)(2,1)S(1)}, u32[]{:S(2)}, u32[]{:S(2)}) collective-permute-start(bf16[192,1024]{1,0:T(8,128)(2,1)} %get-tuple-element.38), channel_id=1, source_target_pairs={{0,1},{1,0},{2,3},{3,2},{4,5},{5,4},{6,7},{7,6},{8,9},{9,8},{10,11... | collective-permute-start | bytes 1179656 | tf_op jit(solution)/shard_map/ppermute | solution.py:366
  64.9 12.8 %copy-start = (bf16[256,256]{1,0:T(8,128)(2,1)S(1)}, bf16[256,256]{1,0:T(8,128)(2,1)}, u32[]{:S(2)}) copy-start(bf16[256,256]{1,0:T(8,128)(2,1)} %constant.11.clone.perm_ref) | copy-start | bytes 393220
  68.1 9.5 %collective-permute-start.5 = (bf16[64,1024]{1,0:T(8,128)(2,1)S(1)}, bf16[64,1024]{1,0:T(8,128)(2,1)S(1)}, u32[]{:S(2)}, u32[]{:S(2)}) collective-permute-start(bf16[64,1024]{1,0:T(8,128)(2,1)S(1)} %get-tuple-element.36), channel_id=1, source_target_pairs={{0,1},{1,0},{2,3},{3,2},{4,5},{5,4},{6,7},{7,6},{8,9},{9,8},{10,11... | collective-permute-start | bytes 393224 | tf_op jit(solution)/shard_map/ppermute | solution.py:366

commit v4 on v3

--- a/solution.py
+++ b/solution.py
@@ -162,11 +162,49 @@
         b64_ref[a] = rows
 
 
-def head_kernel(x_ref, p16_ref, c64_ref, own_ref, dq_ref, part16_ref, part64_ref, stat_ref):
-    def products(kv, qg):
-        both = dot_tt(kv, pair(qg))
-        return both[:, : qg.shape[0]], both[:, qg.shape[0] :]
-
+def products(kv, qg):
+    both = dot_tt(kv, pair(qg))
+    return both[:, : qg.shape[0]], both[:, qg.shape[0] :]
+
+
+def spread(row, width, fill):
+    lines = []
+    for s in range(HEADS):
+        piece = row[:, s * width : (s + 1) * width]
+        if width < DIL:
+            piece = jnp.concatenate([piece, jnp.full((1, DIL - width), fill, F32)], axis=1)
+        lines.append(piece)
+    return jnp.concatenate(lines, axis=0)
+
+
+def segment(x_ref, s):
+    block = x_ref[4 * s : 4 * s + 4, :DIL, :].reshape(4 * DIL, 2 * LANES)
+    return block[:, :LANES], block[:, LANES:]
+
+
+def second_kernel(x_ref, stat_ref):
+    lse, delta = [], []
+    for s in range(2):
+        scores, grad_prob = products(*segment(x_ref, s))
+        got = stats(scores, grad_prob)
+        lse.append(got[2])
+        delta.append(got[3])
+    stat_ref[0] = spread(jnp.concatenate(lse, axis=1), DIL, LOW)
+    stat_ref[1] = spread(jnp.concatenate(delta, axis=1), DIL, 0.0)
+
+
+def third(x_ref, p16_ref):
+    block = x_ref[:, :32, :].reshape(256, 2 * LANES)
+    return jnp.concatenate([block[:, :LANES], p16_ref[...]], axis=0), block[:, LANES:]
+
+
+def third_kernel(x_ref, p16_ref, stat_ref):
+    got = stats(*products(*third(x_ref, p16_ref)))
+    stat_ref[0] = spread(got[2], 32, LOW)
+    stat_ref[1] = spread(got[3], 32, 0.0)
+
+
+def head_kernel(x_ref, second_ref, third_ref, p16_ref, c64_ref, own_ref, dq_ref, part16_ref, part64_ref, stat_ref):
     def grads(kv, qg, scores, grad_prob, lse, delta):
         p = jnp.exp(scores - lse)
         ds = (p * (grad_prob - delta)).astype(BF16)
@@ -174,25 +212,11 @@
         dq = dot((kv * BF16(0.125)).T, ds).T
         return dkv, dq
 
-    def spread(row, width, fill):
-        lines = []
-        for s in range(HEADS):
-            piece = row[:, s * width : (s + 1) * width]
-            if width < DIL:
-                piece = jnp.concatenate([piece, jnp.full((1, DIL - width), fill, F32)], axis=1)
-            lines.append(piece)
-        return jnp.concatenate(lines, axis=0)
-
     def collect(table, width):
         return jnp.concatenate([table[s : s + 1, :width] for s in range(HEADS)], axis=1)
 
-    segments = []
-    for s in range(2):
-        block = x_ref[4 * s : 4 * s + 4, :DIL, :].reshape(4 * DIL, 2 * LANES)
-        segments.append((block[:, :LANES], block[:, LANES:]))
-    block16 = x_ref[:, :32, :].reshape(256, 2 * LANES)
-    kv16 = jnp.concatenate([block16[:, :LANES], p16_ref[...]], axis=0)
-    qg16 = block16[:, LANES:]
+    segments = [segment(x_ref, s) for s in range(2)]
+    kv16, qg16 = third(x_ref, p16_ref)
     qg64 = x_ref[:, :16, LANES:].astype(F32)[:, :8, :].reshape(64, LANES).astype(BF16)
     kv64 = c64_ref[...].reshape(512, LANES)
 
@@ -204,14 +228,11 @@
     lses = [jnp.concatenate(lse1, axis=0)]
     deltas = [jnp.concatenate(delta1, axis=0)]
 
-    made = [products(kv, qg) for kv, qg in segments]
-    got = [stats(*pair) for pair in made]
-    lses.append(spread(jnp.concatenate([got[0][2], got[1][2]], axis=1), DIL, LOW))
-    deltas.append(spread(jnp.concatenate([got[0][3], got[1][3]], axis=1), DIL, 0.0))
+    lses.append(second_ref[0])
+    deltas.append(second_ref[1])
     made16 = products(kv16, qg16)
-    got = stats(*made16)
-    lses.append(spread(got[2], 32, LOW))
-    deltas.append(spread(got[3], 32, 0.0))
+    lses.append(third_ref[0])
+    deltas.append(third_ref[1])
     made64 = products(kv64, qg64)
     got = stats(*made64)
     lses.append(spread(got[2], 8, LOW))
@@ -227,7 +248,7 @@
 
     for s in range(2):
         row = [jnp.concatenate([t[4 * s + i : 4 * s + i + 1] for i in range(4)], axis=1) for t in (lse, delta)]
-        dkv, dq = grads(*segments[s], *made[s], *row)
+        dkv, dq = grads(*segments[s], *products(*segments[s]), *row)
         own_ref[4 * s : 4 * s + 4] = dkv.reshape(4, DIL, LANES)
         dq_ref[4 * s : 4 * s + 4] = dq.reshape(4, DIL, LANES)
     dkv, dq = grads(kv16, qg16, *made16, collect(lse, 32), collect(delta, 32))
@@ -435,6 +456,20 @@
     )(x, weights)
     p16 = swap(mine16, "tm", 8)
     c64 = lax.all_to_all(mine64, "tm", 0, 0, axis_index_groups=across, tiled=True)
+    second = pl.pallas_call(
+        second_kernel,
+        out_shape=shape((2, HEADS, DIL), F32),
+        compiler_params=params(24 * MIB),
+        cost_estimate=cost(2_000_000_000, 4_000_000, 500_000),
+        name="second",
+    )(x)
+    third_stats = pl.pallas_call(
+        third_kernel,
+        out_shape=shape((2, HEADS, DIL), F32),
+        compiler_params=params(24 * MIB),
+        cost_estimate=cost(1_000_000_000, 2_000_000, 130_000),
+        name="third",
+    )(x, p16)
     own, dq_own, part16, part64, stat = pl.pallas_call(
         head_kernel,
         out_shape=[
@@ -446,7 +481,7 @@
         ],
         compiler_params=params(24 * MIB),
         name="heads",
-    )(x, p16, c64)
+    )(x, second, third_stats, p16, c64)
 
     st = stat[None]
     for bit in (1, 2):

time: 79.3 us -> 78.7 us (level)
  waiting for transfers between devices: 14.3 us -> 12.6 us
  Pallas kernels: 29.8 us -> 30.6 us
    pallas_call x0 -> x2, Pallas kernels: none -> 1.4 us  [the longest x1 0.87 us: on_device(): pl.pallas_call(second_kernel, out_shape=shape((2, HEADS, DIL), F32), comp...]
    ppermute x7, waiting for transfers between devices: 10.3 us -> 9.12 us  [swap(): lax.ppermute(x, axis, [(i, i ^ bits) for i in range(lax.axis_size(axis))])]
  transfers between devices with their start and end apart: 11 -> 11, of which waited for: 7 -> 6; matrix products, arithmetic and copies ran while one was open for 0% -> 0% of each run, Pallas kernels for 25% -> 27%
where the time goes in v4:
time: 78.7 us; the launch traced here: 78.2 us
  starting transfers between devices  34.2 us (43%)
  Pallas kernels  30.6 us (39%)
  waiting for transfers between devices  12.6 us (16%)
    ppermute x7, starting transfers between devices, swap(): lax.ppermute(x, axis, [(i, i ^ bits) for i in range(lax.axis_size(axis))])  12.8 us
    pallas_call x1, Pallas kernels, on_device(): pl.pallas_call(local_kernel, grid=(4,), in_specs=[whole((ROWS, ROWS))] +...  10.2 us
    ppermute x7, waiting for transfers between devices, swap(): lax.ppermute(x, axis, [(i, i ^ bits) for i in range(lax.axis_size(axis))])  9.12 us
    all_to_all x1, starting transfers between devices, on_device(): x = lax.all_to_all(sent, 'tm', 0, 0, axis_index_groups=lines, tiled=True)  6.69 us
    all_to_all x1, starting transfers between devices, on_device(): lax.all_to_all(mine64, 'tm', 0, 0, axis_index_groups=across, tiled=True)  5.83 us
    pallas_call x1, Pallas kernels, on_device(): pl.pallas_call(rest_kernel, in_specs=[hbm] * 9, out_specs=[vmem, hbm], ou...  5.57 us
    all_to_all x1, starting transfers between devices, on_device(): got = lax.all_to_all(back, 'tm', 0, 0, axis_index_groups=lines, tiled=True)  5.46 us
    pallas_call x1, Pallas kernels, on_device(): pl.pallas_call(pack_kernel, in_specs=[hbm] * 5, out_specs=hbm, out_shape=...  4.68 us
  transfers between devices with their start and end apart: 11, of which 6 were waited for; matrix products, arithmetic and copies ran while one was open for 0% of the time, Pallas kernels for 27%

profile of v4, /device:TPU:1, one launch (start us, length us, event | category | flops | bytes accessed | tf_op | source)
XLA Modules:
  0.0 78.2 jit_solution(6650666039771041350)
XLA Ops:
  0.0 4.7 %pack.1 = bf16[8,144,256]{2,1,0:T(8,128)(2,1)} custom-call(bf16[128,512]{1,0:T(8,128)(2,1)} %constant.9.clone.perm_hbm, bf16[512,512]{1,0:T(8,128)(2,1)} %q_ref.1, bf16[512,512]{1,0:T(8,128)(2,1)} %k_ref.1, bf16[512,512]{1,0:T(8,128)(2,1)} %v_ref.1, bf16[512,512]{1,0:T(8,128)(2,1)} %g_ref.1), custom_call_target="tpu_custom_call" | custom-call | tf_op jit(solution)/shard_map/pack/pallas_call | solution.py:404
  4.7 6.7 %all-to-all-start = ((bf16[8,144,256]{2,1,0:T(8,128)(2,1)}), bf16[8,144,256]{2,1,0:T(8,128)(2,1)S(1)}, u32[]{:S(2)}, u32[]{:S(2)}) async-start(bf16[8,144,256]{2,1,0:T(8,128)(2,1)} %pack.1), calls=%async_computation | async-start | bytes 1179648 | tf_op jit(solution)/shard_map/all_to_all | solution.py:421
  11.4 10.2 %local.1 = (bf16[2,128,512]{2,1,0:T(8,128)(2,1)}, bf16[2,512,512]{2,1,0:T(8,128)(2,1)}, bf16[384,512]{1,0:T(8,128)(2,1)}, bf16[2,512,512]{2,1,0:T(8,128)(2,1)}, bf16[3,15360,512]{2,1,0:T(8,128)(2,1)}) custom-call(bf16[512,512]{1,0:T(8,128)(2,1)} %constant.8.clone.perm_ref, bf16[512,512]{1,0:T(8,128)(2,1)} %q_ref.1, bf16[512,512]{1,0:T(8,128)(2,1)} %k_ref.1, ...), custom_call_target="tpu_custom_call" | custom-call | flops 12000000000 | bytes 5000000 | tf_op jit(solution)/shard_map/local/pallas_call | solution.py:426
  22.3 5.8 %all-to-all-start.1 = ((bf16[8,64,128]{2,1,0:T(8,128)(2,1)}), bf16[8,64,128]{2,1,0:T(8,128)(2,1)S(1)}, u32[]{:S(2)}, u32[]{:S(2)}) async-start(bf16[8,64,128]{2,1,0:T(8,128)(2,1)} %get-tuple-element.24), calls=%async_computation.1 | async-start | bytes 262144 | tf_op jit(solution)/shard_map/all_to_all | solution.py:458
  28.1 1.5 %collective-permute-start = (bf16[256,128]{1,0:T(8,128)(2,1)S(1)}, bf16[256,128]{1,0:T(8,128)(2,1)S(1)}, u32[]{:S(2)}, u32[]{:S(2)}) collective-permute-start(bf16[256,128]{1,0:T(8,128)(2,1)S(1)} %get-tuple-element.23), channel_id=1, source_target_pairs={{0,16},{2,18},{4,20},{6,22},{8,24},{10,26},{12,28},{14,30},{16,0},... | collective-permute-start | bytes 196616 | tf_op jit(solution)/shard_map/ppermute | solution.py:387
  29.6 0.9 %second.1.second_ref = f32[2,8,128]{2,1,0:T(8,128)S(1)} custom-call(bf16[8,144,256]{2,1,0:T(8,128)(2,1)S(1)} %all-to-all-done.x_ref), custom_call_target="tpu_custom_call" | custom-call | flops 2000000000 | bytes 4000000 | tf_op jit(solution)/shard_map/second/pallas_call | solution.py:459
  30.5 1.2 %collective-permute-done.p16_ref = bf16[256,128]{1,0:T(8,128)(2,1)S(1)} collective-permute-done((bf16[256,128]{1,0:T(8,128)(2,1)S(1)}, bf16[256,128]{1,0:T(8,128)(2,1)S(1)}, u32[]{:S(2)}, u32[]{:S(2)}) %collective-permute-start) | collective-permute-done | bytes 65568 | tf_op jit(solution)/shard_map/ppermute | solution.py:387
  32.2 2.3 %all-to-all-done.1.c64_ref = bf16[8,64,128]{2,1,0:T(8,128)(2,1)S(1)} async-done(((bf16[8,64,128]{2,1,0:T(8,128)(2,1)}), bf16[8,64,128]{2,1,0:T(8,128)(2,1)S(1)}, u32[]{:S(2)}, u32[]{:S(2)}) %all-to-all-start.1) | async-done | bytes 131104 | tf_op jit(solution)/shard_map/all_to_all | solution.py:458
  34.4 2.8 %heads.1 = (f32[8,128,128]{2,1,0:T(8,128)S(1)}, f32[8,128,128]{2,1,0:T(8,128)S(1)}, bf16[256,128]{1,0:T(8,128)(2,1)S(1)}, bf16[8,64,128]{2,1,0:T(8,128)(2,1)}, f32[2,8,128]{2,1,0:T(8,128)S(1)}) custom-call(bf16[8,144,256]{2,1,0:T(8,128)(2,1)S(1)} %all-to-all-done.x_ref, f32[2,8,128]{2,1,0:T(8,128)S(1)} %second.1.second_ref, ...), custom_call_target="tpu_custom_call" | custom-call | tf_op jit(solution)/shard_map/heads/pallas_call | solution.py:473
  37.2 2.1 %collective-permute-start.2 = (f32[1,2,8,128]{3,2,1,0:T(8,128)S(1)}, f32[1,2,8,128]{3,2,1,0:T(8,128)S(1)}, u32[]{:S(2)}, u32[]{:S(2)}) collective-permute-start(f32[1,2,8,128]{3,2,1,0:T(8,128)S(1)} %bitcast.1), channel_id=1, source_target_pairs={{0,2},{2,0},{4,6},{6,4},{8,10},{10,8},{12,14},{14,12},{16,18},{18,... | collective-permute-start | bytes 24584 | tf_op jit(solution)/shard_map/ppermute | solution.py:387
  39.4 3.4 %all-to-all-start.2 = ((bf16[8,64,128]{2,1,0:T(8,128)(2,1)}), bf16[8,64,128]{2,1,0:T(8,128)(2,1)S(1)}, u32[]{:S(2)}, u32[]{:S(2)}) async-start(bf16[8,64,128]{2,1,0:T(8,128)(2,1)} %get-tuple-element.28), calls=%async_computation.2 | async-start | bytes 262144 | tf_op jit(solution)/shard_map/all_to_all | solution.py:491
  42.8 1.0 %collective-permute-start.3 = (f32[2,2,8,128]{3,2,1,0:T(8,128)S(1)}, f32[2,2,8,128]{3,2,1,0:T(8,128)S(1)}, u32[]{:S(2)}, u32[]{:S(2)}) collective-permute-start(f32[2,2,8,128]{3,2,1,0:T(8,128)S(1)} %pad_maximum_fusion.1), channel_id=1, source_target_pairs={{0,4},{2,6},{4,0},{6,2},{8,12},{10,14},{12,8},{14,10},{16,20},{18,... | collective-permute-start | bytes 49160 | tf_op jit(solution)/shard_map/ppermute | solution.py:387
  43.8 1.4 %collective-permute-start.1 = (bf16[256,128]{1,0:T(8,128)(2,1)S(1)}, bf16[256,128]{1,0:T(8,128)(2,1)S(1)}, u32[]{:S(2)}, u32[]{:S(2)}) collective-permute-start(bf16[256,128]{1,0:T(8,128)(2,1)S(1)} %get-tuple-element.27), channel_id=1, source_target_pairs={{0,16},{2,18},{4,20},{6,22},{8,24},{10,26},{12,28},{14,30},{16,0},... | collective-permute-start | bytes 196616 | tf_op jit(solution)/shard_map/ppermute | solution.py:387
  45.5 2.4 %collective-permute-start.4 = (f32[4,2,8,128]{3,2,1,0:T(8,128)S(1)}, f32[4,2,8,128]{3,2,1,0:T(8,128)S(1)}, u32[]{:S(2)}, u32[]{:S(2)}) collective-permute-start(f32[4,2,8,128]{3,2,1,0:T(8,128)S(1)} %pad_maximum_fusion.st_hbm), channel_id=1, source_target_pairs={{0,8},{2,10},{4,12},{6,14},{8,0},{10,2},{12,4},{14,6},{16,24},{18,... | collective-permute-start | bytes 98312 | tf_op jit(solution)/shard_map/ppermute | solution.py:387
  47.9 1.3 %all-to-all-done.2.got64_ref = bf16[8,64,128]{2,1,0:T(8,128)(2,1)S(1)} async-done(((bf16[8,64,128]{2,1,0:T(8,128)(2,1)}), bf16[8,64,128]{2,1,0:T(8,128)(2,1)S(1)}, u32[]{:S(2)}, u32[]{:S(2)}) %all-to-all-start.2) | async-done | bytes 131104 | tf_op jit(solution)/shard_map/all_to_all | solution.py:491
  49.2 0.9 %gather.1 = bf16[8,192,128]{2,1,0:T(8,128)(2,1)} custom-call(f32[8,128,128]{2,1,0:T(8,128)S(1)} %get-tuple-element.25.own_ref, f32[8,128,128]{2,1,0:T(8,128)S(1)} %get-tuple-element.26.dq_ref, bf16[256,128]{1,0:T(8,128)(2,1)S(1)} %collective-permute-done.1.got16_ref, bf16[8,64,128]{2,1,0:T(8,128)(2,1)S(1)} %all-to-all-done.2.got64_ref), custom_call_target="tpu_custom_call" | custom-call | tf_op jit(solution)/shard_map/gather/pallas_call | solution.py:492
  50.1 5.5 %all-to-all-start.3 = ((bf16[8,192,128]{2,1,0:T(8,128)(2,1)}), bf16[8,192,128]{2,1,0:T(8,128)(2,1)S(1)}, u32[]{:S(2)}, u32[]{:S(2)}) async-start(bf16[8,192,128]{2,1,0:T(8,128)(2,1)} %gather.1), calls=%async_computation.3 | async-start | bytes 786432 | tf_op jit(solution)/shard_map/all_to_all | solution.py:498
  56.1 5.6 %rest.1 = (bf16[192,1024]{1,0:T(8,128)(2,1)}, bf16[3,15360,512]{2,1,0:T(8,128)(2,1)}) custom-call(f32[4,2,8,128]{3,2,1,0:T(8,128)} %copy-done.2, f32[4,2,8,128]{3,2,1,0:T(8,128)} %copy-done.3, bf16[2,128,512]{2,1,0:T(8,128)(2,1)} %get-tuple-element.30.in_hbm, bf16[2,512,512]{2,1,0:T(8,128)(2,1)} %get-tuple-element.31.kv_hbm, ...), custom_call_target="tpu_custom_call" | custom-call | flops 5000000000 | bytes 9000000 | tf_op jit(solution)/shard_map/rest/pallas_call | solution.py:501
  61.7 2.5 %collective-permute-start.6 = (bf16[192,1024]{1,0:T(8,128)(2,1)}, bf16[192,1024]{1,0:T(8,128)(2,1)S(1)}, u32[]{:S(2)}, u32[]{:S(2)}) collective-permute-start(bf16[192,1024]{1,0:T(8,128)(2,1)} %get-tuple-element.38), channel_id=1, source_target_pairs={{0,1},{1,0},{2,3},{3,2},{4,5},{5,4},{6,7},{7,6},{8,9},{9,8},{10,11... | collective-permute-start | bytes 1179656 | tf_op jit(solution)/shard_map/ppermute | solution.py:387
  64.3 3.3 %dil.1 = (f32[64,1024]{1,0:T(8,128)S(1)}, bf16[64,1024]{1,0:T(8,128)(2,1)S(1)}, bf16[192,1024]{1,0:T(8,128)(2,1)S(1)}) custom-call(bf16[128,128]{1,0:T(8,128)(2,1)S(1)} %copy-done.1, bf16[8,192,128]{2,1,0:T(8,128)(2,1)S(1)} %all-to-all-done.3.got_ref, bf16[3,15360,512]{2,1,0:T(8,128)(2,1)} %get-tuple-element.34.pass_hbm, ...), custom_call_target="tpu_custom_call" | custom-call | tf_op jit(solution)/shard_map/dil/pallas_call | solution.py:525
  67.5 1.9 %collective-permute-start.5 = (bf16[64,1024]{1,0:T(8,128)(2,1)S(1)}, bf16[64,1024]{1,0:T(8,128)(2,1)S(1)}, u32[]{:S(2)}, u32[]{:S(2)}) collective-permute-start(bf16[64,1024]{1,0:T(8,128)(2,1)S(1)} %get-tuple-element.36), channel_id=1, source_target_pairs={{0,1},{1,0},{2,3},{3,2},{4,5},{5,4},{6,7},{7,6},{8,9},{9,8},{10,11... | collective-permute-start | bytes 393224 | tf_op jit(solution)/shard_map/ppermute | solution.py:387
  69.4 4.8 %collective-permute-done.6.got_r = bf16[192,1024]{1,0:T(8,128)(2,1)S(1)} collective-permute-done((bf16[192,1024]{1,0:T(8,128)(2,1)}, bf16[192,1024]{1,0:T(8,128)(2,1)S(1)}, u32[]{:S(2)}, u32[]{:S(2)}) %collective-permute-start.6) | collective-permute-done | bytes 393248 | tf_op jit(solution)/shard_map/ppermute | solution.py:387
  74.3 2.8 %collective-permute-done.5.got_d = bf16[64,1024]{1,0:T(8,128)(2,1)S(1)} collective-permute-done((bf16[64,1024]{1,0:T(8,128)(2,1)S(1)}, bf16[64,1024]{1,0:T(8,128)(2,1)S(1)}, u32[]{:S(2)}, u32[]{:S(2)}) %collective-permute-start.5) | collective-permute-done | bytes 131104 | tf_op jit(solution)/shard_map/ppermute | solution.py:387
  77.1 1.1 %last.1 = bf16[256,1024]{1,0:T(8,128)(2,1)} custom-call(bf16[256,256]{1,0:T(8,128)(2,1)S(1)} %copy-done, f32[64,1024]{1,0:T(8,128)S(1)} %get-tuple-element.35.keep_d, bf16[64,1024]{1,0:T(8,128)(2,1)S(1)} %collective-permute-done.5.got_d, bf16[192,1024]{1,0:T(8,128)(2,1)S(1)} %get-tuple-element.37.keep_r, bf16[192,1024]{1,0:T(8,128)(2,1)S(1)} %collective-permute-done.6.got_r), custom_call_target="tpu_custom_call" | custom-call | tf_op jit(solution)/shard_map/last/pallas_call | solution.py:539
  (18 shorter events, 2.1 us)
Async XLA Ops:
  4.7 16.9 %all-to-all-start = ((bf16[8,144,256]{2,1,0:T(8,128)(2,1)}), bf16[8,144,256]{2,1,0:T(8,128)(2,1)S(1)}, u32[]{:S(2)}, u32[]{:S(2)}) async-start(bf16[8,144,256]{2,1,0:T(8,128)(2,1)} %pack.1), calls=%async_computation | async-start | bytes 1179648 | tf_op jit(solution)/shard_map/all_to_all | solution.py:421
  21.6 42.6 %copy-start.1 = (bf16[128,128]{1,0:T(8,128)(2,1)S(1)}, bf16[128,128]{1,0:T(8,128)(2,1)}, u32[]{:S(2)}) copy-start(bf16[128,128]{1,0:T(8,128)(2,1)} %constant.10.clone.perm_ref) | copy-start | bytes 98308
  22.3 12.1 %all-to-all-start.1 = ((bf16[8,64,128]{2,1,0:T(8,128)(2,1)}), bf16[8,64,128]{2,1,0:T(8,128)(2,1)S(1)}, u32[]{:S(2)}, u32[]{:S(2)}) async-start(bf16[8,64,128]{2,1,0:T(8,128)(2,1)} %get-tuple-element.24), calls=%async_computation.1 | async-start | bytes 262144 | tf_op jit(solution)/shard_map/all_to_all | solution.py:458
  28.1 3.5 %collective-permute-start = (bf16[256,128]{1,0:T(8,128)(2,1)S(1)}, bf16[256,128]{1,0:T(8,128)(2,1)S(1)}, u32[]{:S(2)}, u32[]{:S(2)}) collective-permute-start(bf16[256,128]{1,0:T(8,128)(2,1)S(1)} %get-tuple-element.23), channel_id=1, source_target_pairs={{0,16},{2,18},{4,20},{6,22},{8,24},{10,26},{12,28},{14,30},{16,0},... | collective-permute-start | bytes 196616 | tf_op jit(solution)/shard_map/ppermute | solution.py:387
  37.2 5.5 %collective-permute-start.2 = (f32[1,2,8,128]{3,2,1,0:T(8,128)S(1)}, f32[1,2,8,128]{3,2,1,0:T(8,128)S(1)}, u32[]{:S(2)}, u32[]{:S(2)}) collective-permute-start(f32[1,2,8,128]{3,2,1,0:T(8,128)S(1)} %bitcast.1), channel_id=1, source_target_pairs={{0,2},{2,0},{4,6},{6,4},{8,10},{10,8},{12,14},{14,12},{16,18},{18,... | collective-permute-start | bytes 24584 | tf_op jit(solution)/shard_map/ppermute | solution.py:387
  39.4 9.8 %all-to-all-start.2 = ((bf16[8,64,128]{2,1,0:T(8,128)(2,1)}), bf16[8,64,128]{2,1,0:T(8,128)(2,1)S(1)}, u32[]{:S(2)}, u32[]{:S(2)}) async-start(bf16[8,64,128]{2,1,0:T(8,128)(2,1)} %get-tuple-element.28), calls=%async_computation.2 | async-start | bytes 262144 | tf_op jit(solution)/shard_map/all_to_all | solution.py:491
  42.8 2.7 %collective-permute-start.3 = (f32[2,2,8,128]{3,2,1,0:T(8,128)S(1)}, f32[2,2,8,128]{3,2,1,0:T(8,128)S(1)}, u32[]{:S(2)}, u32[]{:S(2)}) collective-permute-start(f32[2,2,8,128]{3,2,1,0:T(8,128)S(1)} %pad_maximum_fusion.1), channel_id=1, source_target_pairs={{0,4},{2,6},{4,0},{6,2},{8,12},{10,14},{12,8},{14,10},{16,20},{18,... | collective-permute-start | bytes 49160 | tf_op jit(solution)/shard_map/ppermute | solution.py:387
  43.8 4.1 %collective-permute-start.1 = (bf16[256,128]{1,0:T(8,128)(2,1)S(1)}, bf16[256,128]{1,0:T(8,128)(2,1)S(1)}, u32[]{:S(2)}, u32[]{:S(2)}) collective-permute-start(bf16[256,128]{1,0:T(8,128)(2,1)S(1)} %get-tuple-element.27), channel_id=1, source_target_pairs={{0,16},{2,18},{4,20},{6,22},{8,24},{10,26},{12,28},{14,30},{16,0},... | collective-permute-start | bytes 196616 | tf_op jit(solution)/shard_map/ppermute | solution.py:387
  45.5 10.1 %copy-start.2 = (f32[4,2,8,128]{3,2,1,0:T(8,128)}, f32[4,2,8,128]{3,2,1,0:T(8,128)S(1)}, u32[]{:S(2)}) copy-start(f32[4,2,8,128]{3,2,1,0:T(8,128)S(1)} %pad_maximum_fusion.st_hbm) | copy-start | bytes 98308
  45.5 10.0 %collective-permute-start.4 = (f32[4,2,8,128]{3,2,1,0:T(8,128)S(1)}, f32[4,2,8,128]{3,2,1,0:T(8,128)S(1)}, u32[]{:S(2)}, u32[]{:S(2)}) collective-permute-start(f32[4,2,8,128]{3,2,1,0:T(8,128)S(1)} %pad_maximum_fusion.st_hbm), channel_id=1, source_target_pairs={{0,8},{2,10},{4,12},{6,14},{8,0},{10,2},{12,4},{14,6},{16,24},{18,... | collective-permute-start | bytes 98312 | tf_op jit(solution)/shard_map/ppermute | solution.py:387
  50.1 14.2 %all-to-all-start.3 = ((bf16[8,192,128]{2,1,0:T(8,128)(2,1)}), bf16[8,192,128]{2,1,0:T(8,128)(2,1)S(1)}, u32[]{:S(2)}, u32[]{:S(2)}) async-start(bf16[8,192,128]{2,1,0:T(8,128)(2,1)} %gather.1), calls=%async_computation.3 | async-start | bytes 786432 | tf_op jit(solution)/shard_map/all_to_all | solution.py:498
  55.5 0.6 copy-start.3
  61.7 12.5 %collective-permute-start.6 = (bf16[192,1024]{1,0:T(8,128)(2,1)}, bf16[192,1024]{1,0:T(8,128)(2,1)S(1)}, u32[]{:S(2)}, u32[]{:S(2)}) collective-permute-start(bf16[192,1024]{1,0:T(8,128)(2,1)} %get-tuple-element.38), channel_id=1, source_target_pairs={{0,1},{1,0},{2,3},{3,2},{4,5},{5,4},{6,7},{7,6},{8,9},{9,8},{10,11... | collective-permute-start | bytes 1179656 | tf_op jit(solution)/shard_map/ppermute | solution.py:387
  64.3 12.8 %copy-start = (bf16[256,256]{1,0:T(8,128)(2,1)S(1)}, bf16[256,256]{1,0:T(8,128)(2,1)}, u32[]{:S(2)}) copy-start(bf16[256,256]{1,0:T(8,128)(2,1)} %constant.11.clone.perm_ref) | copy-start | bytes 393220
  67.5 9.5 %collective-permute-start.5 = (bf16[64,1024]{1,0:T(8,128)(2,1)S(1)}, bf16[64,1024]{1,0:T(8,128)(2,1)S(1)}, u32[]{:S(2)}, u32[]{:S(2)}) collective-permute-start(bf16[64,1024]{1,0:T(8,128)(2,1)S(1)} %get-tuple-element.36), channel_id=1, source_target_pairs={{0,1},{1,0},{2,3},{3,2},{4,5},{5,4},{6,7},{7,6},{8,9},{9,8},{10,11... | collective-permute-start | bytes 393224 | tf_op jit(solution)/shard_map/ppermute | solution.py:387
